TPU v7x, 256 devices: a whole 4x4x8 slice. The times are simulated.
256 devices in a mesh: dp: 32 (over y, x, core), tensor: 8 (over z).
Axes of the slice: x: 4, y: 4, z: 8, core: 2. Of those that a mesh axis runs over, the one named last changes fastest.
Arguments:
- pool: bfloat16 [1280, 8, 2, 256, 128], P('dp', 'tensor'), may hold values from -6 to 6
- page_map: int32 [1536], P('dp'), may hold values from 0 to 1279, as said below
- branch_len: int32 [1024], P('dp'), may hold values from 1 to 256
- alive: int32 [1024], P('dp'), may hold values 0 or 1
- queries: bfloat16 [1024, 2, 64, 128], P('dp', None, 'tensor'), may hold values from -20 to 20
- new_keys: bfloat16 [1024, 2, 8, 128], P('dp', None, 'tensor'), may hold values from -8 to 8
- new_values: bfloat16 [1024, 2, 8, 128], P('dp', None, 'tensor'), may hold values from -6 to 6
Outputs:
- attended: bfloat16 [1024, 2, 64, 128], P('dp', None, 'tensor')
Inputs may be any that keep to these rules, and one draw needn't show every extreme that they name: `page_map`: names one pool page for each slot; every pool page is named by one or two slots; the pages of each dp index (page // 40) are named by 48 slots in all; the prompt slots of one block name at most 1 pages of one dp index and its branch slots at most 1, and in every block one dp index is named by exactly 1 prompt slots and 1 branch slots.
All inputs are finite; a program needn't handle non-finite values. No bound on the sum of `alive` on one device may be relied on, other than what follows from the above.
Results may differ from a plain program's by a relative error of at most 0.009.
Values may be sent and summed in bfloat16 or wider, within the bound.
No kernel may reach another device: no remote copies, remote signals or barrier semaphores. Data moves between devices by JAX's collectives and lax.ppermute only.
A program may use at most 64 MiB of HBM per device.

v0:
```python
import jax
import jax.numpy as jnp
from jax import lax
from jax.sharding import PartitionSpec as P

GROUP = 8
PPAGES = 4
BPAGES = 1


NEG = -1e30


def page_partial(question, page_data, live_count):
    blocks, rows_in, step_count, head_count, head_size = question.shape
    kv_heads = page_data.shape[1]
    grouped = question.reshape(
        blocks, rows_in, step_count, kv_heads, head_count // kv_heads, head_size
    )
    scores = jnp.einsum(
        "brskhd,bktd->brskht", grouped, page_data[:, :, 0], preferred_element_type=jnp.float32
    ) * head_size ** (-0.5)
    position = lax.broadcasted_iota(jnp.int32, (1, 1, 1, 1, 1, scores.shape[5]), 5)
    usable = position < live_count[:, :, None, None, None, None]
    masked = jnp.where(usable, scores, NEG)
    highest = jnp.max(masked, axis=5)
    weights = jnp.where(usable, jnp.exp(masked - highest[..., None]), 0.0).astype(jnp.bfloat16)
    weight_sum = jnp.sum(weights.astype(jnp.float32), axis=5)
    blended = jnp.einsum(
        "brskht,bktd->brskhd", weights, page_data[:, :, 1], preferred_element_type=jnp.float32
    )
    return (highest, weight_sum, blended)


def fresh_partial(question, fresh_keys, fresh_values):
    row_count, step_count, head_count, head_size = question.shape
    kv_heads = fresh_keys.shape[2]
    grouped = question.reshape(row_count, step_count, kv_heads, head_count // kv_heads, head_size)
    scores = jnp.einsum(
        "rskhd,rukd->rskhu", grouped, fresh_keys, preferred_element_type=jnp.float32
    ) * head_size ** (-0.5)
    later = lax.broadcasted_iota(jnp.int32, (1, step_count, 1, 1, step_count), 4)
    earlier = lax.broadcasted_iota(jnp.int32, (1, step_count, 1, 1, step_count), 1)
    usable = later <= earlier
    masked = jnp.where(usable, scores, NEG)
    highest = jnp.max(masked, axis=4)
    weights = jnp.where(usable, jnp.exp(masked - highest[..., None]), 0.0).astype(jnp.bfloat16)
    weight_sum = jnp.sum(weights.astype(jnp.float32), axis=4)
    blended = jnp.einsum(
        "rskhu,rukd->rskhd", weights, fresh_values, preferred_element_type=jnp.float32
    )
    return (highest, weight_sum, blended)


def arrange(prompt_piece, branch_piece, fresh_piece, groups):
    row_count = fresh_piece.shape[0]
    prompt_rows = prompt_piece.reshape((groups, PPAGES) + prompt_piece.shape[1:])
    prompt_rows = jnp.swapaxes(prompt_rows, 1, 2).reshape(
        (row_count, PPAGES) + prompt_piece.shape[2:]
    )
    branch_rows = branch_piece[:, 0].reshape((row_count, BPAGES) + branch_piece.shape[2:])
    return jnp.concatenate([prompt_rows, branch_rows, fresh_piece[:, None]], axis=1)


def finish(highs, sums, blends, alive):
    ceiling = jnp.max(highs, axis=1, keepdims=True)
    factor = jnp.exp(highs - ceiling)
    weight_sum = jnp.sum(factor * sums, axis=1)
    blended = jnp.sum(factor[..., None] * blends, axis=1)
    result = blended / weight_sum[..., None] * alive.astype(jnp.float32)[:, None, None, None, None]
    row_count, step_count, kv_heads, per_head, head_size = result.shape
    return result.reshape(row_count, step_count, kv_heads * per_head, head_size).astype(
        jnp.bfloat16
    )


def slot_rank(source):
    width = source.shape[-1]
    before = lax.broadcasted_iota(jnp.int32, (width, width), 1) < lax.broadcasted_iota(
        jnp.int32, (width, width), 0
    )
    same_source = source[..., :, None] == source[..., None, :]
    return jnp.sum(jnp.where(same_source & before, 1, 0), axis=-1).astype(jnp.int32)


def shards(pool, page_map, branch_len, alive, queries, new_keys, new_values):
    partners = lax.axis_size("dp")
    my_index = lax.axis_index("dp")
    pool_row = pool.shape[0]
    page_size = pool.shape[3]
    slot_count = page_map.shape[0]
    row_count = queries.shape[0]
    groups = row_count // GROUP
    prompt_slots = groups * PPAGES
    branch_slots = row_count * BPAGES
    prompt_cap = (prompt_slots + partners - 1) // partners
    branch_cap = (branch_slots + partners - 1) // partners
    capacity = prompt_cap + branch_cap
    source = page_map // pool_row
    grouped = queries.reshape((groups, 1, GROUP) + queries.shape[1:])
    prompt_question = jnp.broadcast_to(
        grouped, (groups, PPAGES, GROUP) + queries.shape[1:]
    ).reshape((prompt_slots, GROUP) + queries.shape[1:])
    prompt_count = jnp.full((prompt_slots, GROUP), page_size, jnp.int32)
    branch_question = queries[:, None]
    offsets = jnp.arange(BPAGES, dtype=jnp.int32) * page_size
    branch_count = jnp.clip(branch_len[:, None] - offsets[None, :], 0, page_size)
    arrival = slot_rank(source)
    landing = source * capacity + arrival
    place_ids = jnp.arange(capacity, dtype=jnp.int32)[None, :, None]
    everyone = lax.all_gather(page_map, "dp", axis=0, tiled=True).reshape(partners, slot_count)
    owners = everyone // pool_row
    picks = (owners == my_index)[:, None, :] & (slot_rank(owners)[:, None, :] == place_ids)
    chosen = jnp.sum(jnp.where(picks, (everyone % pool_row)[:, None, :], 0), axis=2)
    outgoing = pool[chosen.reshape(-1)].reshape((partners, capacity) + pool.shape[1:])
    incoming = lax.all_to_all(outgoing, "dp", split_axis=0, concat_axis=0, tiled=True)
    placed = incoming.reshape((partners * capacity,) + pool.shape[1:])[landing]
    prompt_part = page_partial(prompt_question, placed[:prompt_slots], prompt_count)
    branch_part = page_partial(branch_question, placed[prompt_slots:], branch_count)
    fresh_part = fresh_partial(queries, new_keys, new_values)
    highs = arrange(prompt_part[0], branch_part[0], fresh_part[0], groups)
    sums = arrange(prompt_part[1], branch_part[1], fresh_part[1], groups)
    blends = arrange(prompt_part[2], branch_part[2], fresh_part[2], groups)
    return finish(highs, sums, blends, alive)


def solution(mesh):
    return jax.shard_map(
        shards,
        mesh=mesh,
        in_specs=(
            P("dp", "tensor", None, None, None),
            P("dp"),
            P("dp"),
            P("dp"),
            P("dp", None, "tensor", None),
            P("dp", None, "tensor", None),
            P("dp", None, "tensor", None),
        ),
        out_specs=P("dp", None, "tensor", None),
        check_vma=False,
    )
```

profile of v0, /device:TPU:32, one launch (start us, length us, event | category | flops | bytes accessed | tf_op | source)
XLA Modules:
  0.0 174.6 jit_solution(1171186811813695250)
XLA Ops:
  0.0 1.3 dynamic-slice
  2.0 0.9 dynamic-update-slice
  2.8 17.1 %all-reduce = s32[1536]{0:T(1024)S(1)} all-reduce(s32[1536]{0:T(1024)S(1)} %dynamic-update-slice), channel_id=1, replica_groups=mesh['dp'=32,'tensor'=8] {'dp'}, use_global_device_ids=true, to_apply=%add | all-reduce | flops 1536 | bytes 12288
  20.0 0.1 rem.41
  20.1 0.1 div.38
  20.2 0.1 ne.72
  20.3 0.8 select_reduce_fusion
  21.1 0.1 select_reduce_fusion.1
  21.2 0.1 copy.57
  21.3 0.1 reshape.469
  21.5 8.0 %gather_fusion = bf16[64,2,256,128]{3,2,1,0:T(8,128)(2,1)} fusion(bf16[40,2,256,128]{3,2,1,0:T(8,128)(2,1)} %bitcast.166, s32[1024]{0:T(1024)S(1)} %pad_clamp_fusion.1), kind=kCustom, calls=%fused_computation | custom fusion | bytes 16777472 | tf_op jit(solution)/shard_map/gather | solution.py:115
  29.5 5.1 %all-to-all-start = ((bf16[32,2,1,2,256,128]{5,4,3,1,2,0:T(8,128)(2,1)}), bf16[32,2,1,2,256,128]{5,4,3,1,2,0:T(8,128)(2,1)}, u32[]{:S(2)}, u32[]{:S(2)}) async-start(bf16[32,2,1,2,256,128]{5,4,3,1,2,0:T(8,128)(2,1)} %bitcast.165), calls=%async_computation | async-start | bytes 16777216 | tf_op jit(solution)/shard_map/all_to_all | solution.py:116
  34.6 0.7 fusion.29
  35.4 0.2 convert_reduce_fusion.2
  35.5 0.1 copy.76
  35.7 0.7 copy.62
  36.4 0.5 convert_element_type.30
  36.9 0.2 select_reduce_fusion.2
  37.1 0.9 convolution_bitcast_fusion
  38.0 0.1 iota_compare_fusion
  38.1 102.4 %all-to-all-done = bf16[32,2,1,2,256,128]{5,4,3,1,2,0:T(8,128)(2,1)} async-done(((bf16[32,2,1,2,256,128]{5,4,3,1,2,0:T(8,128)(2,1)}), bf16[32,2,1,2,256,128]{5,4,3,1,2,0:T(8,128)(2,1)}, u32[]{:S(2)}, u32[]{:S(2)}) %all-to-all-start) | async-done | bytes 8388640 | tf_op jit(solution)/shard_map/all_to_all | solution.py:116
  140.5 8.4 %gather_fusion.1 = bf16[48,2,256,128]{3,2,1,0:T(8,128)(2,1)} fusion(bf16[64,2,256,128]{3,2,1,0:T(8,128)(2,1)} %bitcast.4, s32[1024]{0:T(1024)S(1)} %pad_clamp_fusion), kind=kCustom, calls=%fused_computation.1 | custom fusion | bytes 12583104 | tf_op jit(solution)/shard_map/gather | solution.py:117
  148.9 3.2 %copy.85 = bf16[48,2,256,128]{3,2,0,1:T(8,128)(2,1)S(1)} copy(bf16[48,2,256,128]{3,2,1,0:T(8,128)(2,1)} %gather_fusion.1) | data formatting | bytes 12582912 | tf_op jit(solution)/shard_map/gather | solution.py:117
  152.1 0.1 broadcast_in_dim.129
  152.2 2.5 %copy-done.1 = bf16[48,2,256,128]{3,2,0,1:T(8,128)(2,1)} copy-done((bf16[48,2,256,128]{3,2,0,1:T(8,128)(2,1)}, bf16[48,2,256,128]{3,2,0,1:T(8,128)(2,1)S(1)}, u32[]{:S(2)}) %copy-start.1) | copy-done | bytes 6291480
  154.7 0.7 bitcast_reduce_fusion
  155.5 0.1 copy.60
  155.6 0.7 concatenate.69
  156.3 0.7 concatenate.62
  157.1 2.3 %fusion.30 = (f32[32,2,8]{2,1,0:T(2,128)S(1)}, f32[32,1,2,1,8,256]{5,4,2,0,1,3:T(8,128)S(1)}) fusion(bf16[32,2,8,128]{3,2,1,0:T(8,128)(2,1)S(1)} %copy-done, bf16[48,1,2,256,128]{4,3,0,2,1:T(8,128)(2,1)} %bitcast.168, pred[32,256]{1,0:T(8,128)(4,1)S(1)} %iota_compare_fusion), kind=kOutput, calls=%fused_computation.72 | convolution fusion | flops 33947136 | bytes 2762752 | tf_op jit(solution)/shard_map/brskhd,bktd->brskht/dot_general | solution.py:20
  159.4 0.9 convert_reduce_fusion.1
  160.3 2.8 %fusion.10 = f32[32,1,2,1,8,128]{5,4,2,1,0,3:T(8,128)} fusion(bf16[48,1,2,256,128]{4,3,0,2,1:T(8,128)(2,1)} %bitcast.169, f32[32,1,2,1,8,256]{5,4,2,0,1,3:T(8,128)S(1)} %get-tuple-element.14, f32[32,2,8]{2,1,0:T(2,128)S(1)} %get-tuple-element.13, pred[32,256]{1,0:T(8,128)(4,1)S(1)} %iota_compare_fusion), kind=kOutput, calls=%fused_computation.20 | convolution fusion | flops 33947648 | bytes 2893824 | tf_op jit(solution)/shard_map/brskht,bktd->brskhd/dot_general | solution.py:29
  163.1 1.7 convert_reduce_fusion
  164.8 1.8 %fusion.13 = f32[16,128,8,2,8]{1,4,3,2,0:T(8,128)S(1)} fusion(bf16[48,1,2,256,128]{4,3,0,2,1:T(8,128)(2,1)} %bitcast.170, f32[16,256,8,2,8]{1,4,3,2,0:T(8,128)S(1)} %get-tuple-element.16, f32[16,8,2,8]{3,2,1,0:T(2,128)S(1)} %get-tuple-element.15, pred[256]{0:T(512)(128)(4,1)} %copy-done.7), kind=kOutput, calls=%fused_computation.26 | convolution fusion | flops 136839168 | bytes 4203520 | tf_op jit(solution)/shard_map/brskht,bktd->brskhd/dot_general | solution.py:29
  166.7 0.8 fusion.22
  167.6 0.8 copy.75
  168.4 0.9 copy.73
  169.3 0.1 copy.74
  169.5 0.1 concatenate.73
  169.6 0.8 copy.70
  170.4 0.8 fusion.20
  171.2 0.1 copy.77
  171.3 0.8 copy.61
  172.1 0.8 fusion.17
  172.9 0.2 copy.65
  173.1 0.1 copy.66
  173.2 0.5 fusion.5
  173.7 0.8 multiply_convert_fusion
  (44 shorter events, 0.4 us)
Async XLA Ops:
  0.0 34.6 %copy-start = (bf16[32,2,8,128]{3,2,1,0:T(8,128)(2,1)S(1)}, bf16[32,2,8,128]{3,2,1,0:T(8,128)(2,1)}, u32[]{:S(2)}) copy-start(bf16[32,2,8,128]{3,2,1,0:T(8,128)(2,1)} %param.11) | copy-start | bytes 393220
  29.5 5.2 %copy-start.9 = (bf16[32,2,1,128]{3,1,2,0:T(2,128)(2,1)S(1)}, bf16[32,2,1,128]{3,1,2,0:T(2,128)(2,1)}, u32[]{:S(2)}) copy-start(bf16[32,2,1,128]{3,1,2,0:T(2,128)(2,1)} %param.12) | copy-start | bytes 49156
  29.5 6.9 %copy-start.10 = (s32[32]{0:T(128)S(1)}, s32[32]{0:T(128)}, u32[]{:S(2)}) copy-start(s32[32]{0:T(128)} %param.10) | copy-start | bytes 388
  29.5 7.4 %copy-start.11 = (s32[48]{0:T(128)S(1)}, s32[48]{0:T(128)}, u32[]{:S(2)}) copy-start(s32[48]{0:T(128)} %param.8) | copy-start | bytes 580
  29.5 7.6 %copy-start.6 = (bf16[32,2,1,128]{3,1,2,0:T(2,128)(2,1)S(1)}, bf16[32,2,1,128]{3,1,2,0:T(2,128)(2,1)}, u32[]{:S(2)}) copy-start(bf16[32,2,1,128]{3,1,2,0:T(2,128)(2,1)} %param.13) | copy-start | bytes 49156
  29.5 8.6 %copy-start.12 = (s32[32]{0:T(128)S(1)}, s32[32]{0:T(128)}, u32[]{:S(2)}) copy-start(s32[32]{0:T(128)} %param.9) | copy-start | bytes 388
  29.5 111.0 %all-to-all-start = ((bf16[32,2,1,2,256,128]{5,4,3,1,2,0:T(8,128)(2,1)}), bf16[32,2,1,2,256,128]{5,4,3,1,2,0:T(8,128)(2,1)}, u32[]{:S(2)}, u32[]{:S(2)}) async-start(bf16[32,2,1,2,256,128]{5,4,3,1,2,0:T(8,128)(2,1)} %bitcast.165), calls=%async_computation | async-start | bytes 16777216 | tf_op jit(solution)/shard_map/all_to_all | solution.py:116
  35.3 113.5 %copy-start.3 = (f32[32,2,8]{2,1,0:T(2,128)}, f32[32,2,8]{2,1,0:T(2,128)S(1)}, u32[]{:S(2)}) copy-start(f32[32,2,8]{2,1,0:T(2,128)S(1)} %get-tuple-element.11) | copy-start | bytes 6148
  36.8 126.2 %copy-start.7 = (pred[256]{0:T(512)(128)(4,1)}, pred[256]{0:T(512)(128)(4,1)S(1)}, u32[]{:S(2)}) copy-start(pred[256]{0:T(512)(128)(4,1)S(1)} %iota_compare_fusion.4) | copy-start | bytes 772
  152.1 2.7 %copy-start.1 = (bf16[48,2,256,128]{3,2,0,1:T(8,128)(2,1)}, bf16[48,2,256,128]{3,2,0,1:T(8,128)(2,1)S(1)}, u32[]{:S(2)}) copy-start(bf16[48,2,256,128]{3,2,0,1:T(8,128)(2,1)S(1)} %copy.85) | copy-start | bytes 18874372
  159.4 3.7 %copy-start.4 = (f32[32,2,8]{2,1,0:T(2,128)}, f32[32,2,8]{2,1,0:T(2,128)S(1)}, u32[]{:S(2)}) copy-start(f32[32,2,8]{2,1,0:T(2,128)S(1)} %get-tuple-element.13) | copy-start | bytes 6148
  166.6 6.6 %copy-start.2 = (f32[32,1,2,1,8,128]{5,4,2,1,0,3:T(8,128)S(1)}, f32[32,1,2,1,8,128]{5,4,2,1,0,3:T(8,128)}, u32[]{:S(2)}) copy-start(f32[32,1,2,1,8,128]{5,4,2,1,0,3:T(8,128)} %convolution_bitcast_fusion) | copy-start | bytes 786436
  166.6 6.6 %copy-start.5 = (f32[32,1,2,1,8,128]{5,4,2,1,0,3:T(8,128)S(1)}, f32[32,1,2,1,8,128]{5,4,2,1,0,3:T(8,128)}, u32[]{:S(2)}) copy-start(f32[32,1,2,1,8,128]{5,4,2,1,0,3:T(8,128)} %fusion.10) | copy-start | bytes 786436
  173.1 0.7 copy-start.8
where the time goes:
time: 175 us
  waiting for transfers between devices  102 us (58%)
  local copies, waits for them, and re-layouts  31.3 us (18%)
  blocking collectives  17.1 us (10%)
  matrix products  9.31 us (5%)
  other arithmetic  8.34 us (5%)
  starting transfers between devices  5.1 us (3%)
    all_to_all x1, waiting for transfers between devices, shards(): lax.all_to_all(outgoing, 'dp', split_axis=0, concat_axis=0, tiled=True)  102 us
    unnamed x1, blocking collectives  17.1 us
    gather x2, local copies, waits for them, and re-layouts, shards(): placed = incoming.reshape((partners * capacity,) + pool.shape[1:])[landing]  11.6 us
    gather x1, local copies, waits for them, and re-layouts, shards(): pool[chosen.reshape(-1)].reshape((partners, capacity) + pool.shape[1:])  7.98 us
    all_to_all x1, starting transfers between devices, shards(): lax.all_to_all(outgoing, 'dp', split_axis=0, concat_axis=0, tiled=True)  5.1 us
    concatenate x9, local copies, waits for them, and re-layouts, arrange(): jnp.concatenate([prompt_rows, branch_rows, fresh_piece[:, None]], axis=1)  4.86 us
    unnamed x29, local copies, waits for them, and re-layouts  4.77 us
    dot_general x2, matrix products, page_partial(): jnp.einsum('brskht,bktd->brskhd', weights, page_data[:, :, 1], preferred_...  4.61 us
  transfers between devices with their start and end apart: 1, of which 1 were waited for; matrix products, arithmetic and copies ran while one was open for 2% of the time, Pallas kernels for 0%

commit v1 on v0

v1 whole, which is shorter than its diff:
```python
import jax
import jax.numpy as jnp
from jax import lax
from jax.experimental import pallas as pl
from jax.experimental.pallas import tpu as pltpu
from jax.sharding import PartitionSpec as P

GROUP = 8
PPAGES = 4
POOL_ROW = 40
PAGE = 256
HD = 128
DP = 32
ROWS_DEV = 32
SH = 16
PROMPTS = 16
BRANCH_AT = GROUP * SH
TAIL_AT = BRANCH_AT + SH
MSG = TAIL_AT + SH
NEG = -1e30
LN2 = 0.6931471805599453
SCALE = HD ** (-0.5)
TO_LOG2 = SCALE / LN2
BF = jnp.bfloat16
F32 = jnp.float32
CONTRACT_LAST = (((1,), (1,)), ((), ()))
VMEM = pl.BlockSpec(memory_space=pltpu.VMEM)
SMEM = pl.BlockSpec(memory_space=pltpu.SMEM)
PARAMS = pltpu.CompilerParams(vmem_limit_bytes=40 * 1024 * 1024)


def pack_kernel(map_ref, len_ref, q_ref, out_ref, held_ref):
    lane = lax.broadcasted_iota(jnp.int32, (SH, HD), 1)
    for s in range(DP):
        held_ref[s] = -1
    for j in range(PROMPTS):
        page = map_ref[j]
        s = page // POOL_ROW
        held_ref[s] = page - s * POOL_ROW
        g = j // PPAGES
        for i in range(GROUP):
            out_ref[s, i * SH : (i + 1) * SH, :] = q_ref[g * GROUP + i]
    for e in range(ROWS_DEV):
        page = map_ref[PROMPTS + e]
        s = page // POOL_ROW
        out_ref[s, BRANCH_AT:TAIL_AT, :] = q_ref[e]
        numbers = jnp.where(
            lane == 0, held_ref[s], jnp.where(lane == 1, page - s * POOL_ROW, len_ref[e])
        )
        out_ref[s, TAIL_AT:MSG, :] = numbers.astype(F32).astype(BF)


def attend_kernel(in_ref, pool_ref, out_ref, numbers_v, numbers_s, list_s, stats, sem):
    lane = lax.broadcasted_iota(jnp.int32, (SH, HD), 1)
    token = lax.broadcasted_iota(jnp.int32, (SH, PAGE), 1)
    for b in range(DP):
        numbers_v[b : b + 1, :] = in_ref[b, TAIL_AT:MSG, :].astype(F32)[0:1].astype(jnp.int32)
    copy = pltpu.make_async_copy(numbers_v, numbers_s, sem)
    copy.start()
    stats[...] = jnp.zeros_like(stats)
    copy.wait()
    count = jnp.int32(0)
    for b in range(DP):
        list_s[count] = b
        count = count + jnp.where(numbers_s[b, 0] >= 0, 1, 0)

    def partial(question, page, usable):
        keys = pool_ref[page, 0]
        values = pool_ref[page, 1]
        scores = lax.dot_general(question, keys, CONTRACT_LAST, preferred_element_type=F32)
        if usable is not None:
            scores = jnp.where(usable, scores, NEG)
        highest = jnp.max(scores, axis=1, keepdims=True)
        weights = jnp.exp2((scores - highest) * TO_LOG2).astype(BF)
        total = jnp.sum(weights.astype(F32), axis=1, keepdims=True)
        mix = jnp.dot(weights, values, preferred_element_type=F32)
        return (mix / total).astype(BF), highest * SCALE + jnp.log(total)

    def prompt(j, carry):
        b = list_s[j]
        mix, lse = partial(in_ref[b, 0:BRANCH_AT, :], numbers_s[b, 0], None)
        out_ref[b, 0:BRANCH_AT, :] = mix
        tile = jnp.zeros((SH, HD), F32)
        for i in range(GROUP):
            tile = jnp.where(lane == i, lse[i * SH : (i + 1) * SH], tile)
        stats[b] = tile
        return carry

    lax.fori_loop(0, PROMPTS, prompt, 0, unroll=4)

    def branch(b, carry):
        length = in_ref[b, TAIL_AT:MSG, :].astype(F32)[:, 2:3].astype(jnp.int32)
        mix, lse = partial(in_ref[b, BRANCH_AT:TAIL_AT, :], numbers_s[b, 1], token < length)
        out_ref[b, BRANCH_AT:TAIL_AT, :] = mix
        tile = jnp.where(lane == GROUP, lse, stats[b])
        high = tile.astype(BF).astype(F32)
        rest = tile - high
        middle = rest.astype(BF).astype(F32)
        low = rest - middle
        out_ref[b, TAIL_AT:MSG, :] = (
            high + pltpu.roll(middle, 16, 1) + pltpu.roll(low, 32, 1)
        ).astype(BF)
        return carry

    lax.fori_loop(0, DP, branch, 0, unroll=8)


def combine_kernel(map_ref, alive_ref, in_ref, q_ref, nk_ref, nv_ref, out_ref, fresh_ref):
    lane = lax.broadcasted_iota(jnp.int32, (SH, HD), 1)
    width = nk_ref.shape[0]
    question = q_ref[...].reshape(ROWS_DEV * SH, HD)
    scores = lax.dot_general(question, nk_ref[...], CONTRACT_LAST, preferred_element_type=F32)
    at = lax.broadcasted_iota(jnp.int32, scores.shape, 0)
    new = lax.broadcasted_iota(jnp.int32, scores.shape, 1)
    usable = (at // SH == new // 2) & (new % 2 <= (at % SH) // (SH // 2))
    scores = jnp.where(usable, scores, NEG)
    highest = jnp.max(scores, axis=1, keepdims=True)
    weights = jnp.where(usable, jnp.exp2((scores - highest) * TO_LOG2), 0.0).astype(BF)
    total = jnp.sum(weights.astype(F32), axis=1, keepdims=True)
    mix = jnp.dot(weights, nv_ref[...], preferred_element_type=F32)
    fresh_ref[...] = (mix / total).reshape(ROWS_DEV, SH, HD)
    fresh_lse = highest * SCALE + jnp.log(total)

    def numbers(s):
        tile = in_ref[s, TAIL_AT:MSG, :].astype(F32)
        return tile + pltpu.roll(tile, HD - 16, 1) + pltpu.roll(tile, HD - 32, 1)

    for g in range(ROWS_DEV // GROUP):
        holders = [map_ref[g * PPAGES + k] // POOL_ROW for k in range(PPAGES)]
        levels = [numbers(s) for s in holders]
        own, fresh = jnp.zeros((SH, HD), F32), jnp.zeros((SH, HD), F32)
        homes = []
        for i in range(GROUP):
            row = g * GROUP + i
            s = map_ref[PROMPTS + row] // POOL_ROW
            homes.append(s)
            own = jnp.where(lane == i, numbers(s)[:, GROUP : GROUP + 1], own)
            fresh = jnp.where(lane == i, fresh_lse[row * SH : (row + 1) * SH], fresh)
        levels = levels + [own, fresh]
        peak = levels[0]
        for level in levels[1:]:
            peak = jnp.maximum(peak, level)
        shares = [jnp.exp(level - peak) for level in levels]
        whole = shares[0]
        for share in shares[1:]:
            whole = whole + share
        shares = [share / whole for share in shares]
        for i in range(GROUP):
            row = g * GROUP + i
            parts = [in_ref[s, i * SH : (i + 1) * SH, :].astype(F32) for s in holders]
            parts.append(in_ref[homes[i], BRANCH_AT:TAIL_AT, :].astype(F32))
            parts.append(fresh_ref[row])
            result = shares[0][:, i : i + 1] * parts[0]
            for share, part in zip(shares[1:], parts[1:]):
                result = result + share[:, i : i + 1] * part
            out_ref[row] = (result * alive_ref[row].astype(F32)).astype(BF)


def exchange(message):
    return lax.all_to_all(message, "dp", split_axis=0, concat_axis=0, tiled=True)


def shards(pool, page_map, branch_len, alive, queries, new_keys, new_values):
    message = jax.ShapeDtypeStruct((DP, MSG, HD), BF)
    question = queries.reshape(ROWS_DEV, SH, HD)
    pages = pool.reshape(POOL_ROW, 2, PAGE, HD)
    outgoing = pl.pallas_call(
        pack_kernel,
        out_shape=message,
        in_specs=[SMEM, SMEM, VMEM],
        out_specs=VMEM,
        scratch_shapes=[pltpu.SMEM((DP,), jnp.int32)],
        compiler_params=PARAMS,
        name="pack",
    )(page_map, branch_len, question)
    asked = exchange(outgoing)
    answers = pl.pallas_call(
        attend_kernel,
        out_shape=message,
        in_specs=[VMEM, VMEM],
        out_specs=VMEM,
        scratch_shapes=[
            pltpu.VMEM((DP, HD), jnp.int32),
            pltpu.SMEM((DP, HD), jnp.int32),
            pltpu.SMEM((DP + 8,), jnp.int32),
            pltpu.VMEM((DP, SH, HD), F32),
            pltpu.SemaphoreType.DMA,
        ],
        compiler_params=PARAMS,
        name="attend",
    )(asked, pages)
    incoming = exchange(answers)
    attended = pl.pallas_call(
        combine_kernel,
        out_shape=jax.ShapeDtypeStruct((ROWS_DEV, SH, HD), BF),
        in_specs=[SMEM, SMEM, VMEM, VMEM, VMEM, VMEM],
        out_specs=VMEM,
        scratch_shapes=[pltpu.VMEM((ROWS_DEV, SH, HD), F32)],
        compiler_params=PARAMS,
        name="combine",
    )(
        page_map,
        alive,
        incoming,
        question,
        new_keys.reshape(ROWS_DEV * 2, HD),
        new_values.reshape(ROWS_DEV * 2, HD),
    )
    return attended.reshape(queries.shape)


def solution(mesh):
    return jax.shard_map(
        shards,
        mesh=mesh,
        in_specs=(
            P("dp", "tensor", None, None, None),
            P("dp"),
            P("dp"),
            P("dp"),
            P("dp", None, "tensor", None),
            P("dp", None, "tensor", None),
            P("dp", None, "tensor", None),
        ),
        out_specs=P("dp", None, "tensor", None),
        check_vma=False,
    )
```

time: 175 us -> 74.2 us (0.42)
  the two profiles are of different devices: /device:TPU:32 before, /device:TPU:1 now
where the time goes in v1:
time: 74.2 us; the launch traced here: 74 us
  blocking collectives  52.4 us (71%)
  Pallas kernels  16.8 us (23%)
  local copies, waits for them, and re-layouts  4.72 us (6%)
    all_to_all x2, blocking collectives, exchange(): lax.all_to_all(message, 'dp', split_axis=0, concat_axis=0, tiled=True)  52.4 us
    pallas_call x1, Pallas kernels, shards(): pl.pallas_call(attend_kernel, out_shape=message, in_specs=[VMEM, VMEM], o...  11.9 us
    unnamed x16, local copies, waits for them, and re-layouts  4.72 us
    pallas_call x1, Pallas kernels, shards(): pl.pallas_call(combine_kernel, out_shape=jax.ShapeDtypeStruct((ROWS_DEV,...  4 us

profile of v1, /device:TPU:1, one launch (start us, length us, event | category | flops | bytes accessed | tf_op | source)
XLA Modules:
  0.0 74.0 jit_solution(15865883281802042086)
XLA Ops:
  0.0 0.0 copy-start.1
  0.0 0.9 %copy-done.1 = bf16[32,2,8,128]{3,2,1,0:T(8,128)(2,1)S(1)} copy-done((bf16[32,2,8,128]{3,2,1,0:T(8,128)(2,1)S(1)}, bf16[32,2,8,128]{3,2,1,0:T(8,128)(2,1)}, u32[]{:S(2)}) %copy-start.1) | copy-done | bytes 131096
  0.9 0.0 copy-start.5
  0.9 0.7 copy-done.5
  1.6 0.0 copy-start.6
  1.6 0.7 copy-done.6
  2.2 0.9 %pack.1 = bf16[32,160,128]{2,1,0:T(8,128)(2,1)S(1)} custom-call(s32[48]{0:T(128)S(1)} %copy-done.5, s32[32]{0:T(128)S(1)} %copy-done.6, bf16[32,16,128]{2,1,0:T(8,128)(2,1)S(1)} %bitcast.6), custom_call_target="tpu_custom_call" | custom-call | tf_op jit(solution)/shard_map/pack/pallas_call | solution.py:167
  3.1 28.6 %all_to_all.10.in_ref = bf16[32,160,128]{2,1,0:T(8,128)(2,1)S(1)} all-to-all(bf16[32,160,128]{2,1,0:T(8,128)(2,1)S(1)} %pack.1), channel_id=1, replica_groups=mesh['dp'=32,'tensor'=8] {'dp'}, dimensions={0} | all-to-all | bytes 2621440 | tf_op jit(solution)/shard_map/all_to_all | solution.py:160
  31.7 0.0 copy-start
  31.7 2.5 %copy-done = bf16[40,1,2,256,128]{4,3,2,1,0:T(8,128)(2,1)S(1)} copy-done((bf16[40,1,2,256,128]{4,3,2,1,0:T(8,128)(2,1)S(1)}, bf16[40,1,2,256,128]{4,3,2,1,0:T(8,128)(2,1)}, u32[]{:S(2)}) %copy-start) | copy-done | bytes 5242904
  34.2 11.9 %attend.1 = bf16[32,160,128]{2,1,0:T(8,128)(2,1)S(1)} custom-call(bf16[32,160,128]{2,1,0:T(8,128)(2,1)S(1)} %all_to_all.10.in_ref, bf16[40,2,256,128]{3,2,1,0:T(8,128)(2,1)S(1)} %bitcast.5), custom_call_target="tpu_custom_call" | custom-call | tf_op jit(solution)/shard_map/attend/pallas_call | solution.py:177
  46.1 0.0 copy-start.2
  46.1 0.0 copy-start.3
  46.1 0.0 copy-start.4
  46.1 0.0 copy-start.7
  46.1 23.8 %all_to_all.11.in_ref = bf16[32,160,128]{2,1,0:T(8,128)(2,1)S(1)} all-to-all(bf16[32,160,128]{2,1,0:T(8,128)(2,1)S(1)} %attend.1), channel_id=1, replica_groups=mesh['dp'=32,'tensor'=8] {'dp'}, dimensions={0} | all-to-all | bytes 2621440 | tf_op jit(solution)/shard_map/all_to_all | solution.py:160
  69.9 0.0 copy-done.2
  69.9 0.0 copy-done.3
  69.9 0.0 copy-done.4
  69.9 0.0 copy-done.7
  70.0 4.0 %combine.1 = bf16[32,16,128]{2,1,0:T(8,128)(2,1)} custom-call(s32[48]{0:T(128)S(1)} %copy-done.5, s32[32]{0:T(128)S(1)} %copy-done.7, bf16[32,160,128]{2,1,0:T(8,128)(2,1)S(1)} %all_to_all.11.in_ref, bf16[32,16,128]{2,1,0:T(8,128)(2,1)S(1)} %bitcast.7, bf16[64,128]{1,0:T(8,128)(2,1)S(1)} %bitcast.8, bf16[64,128]{1,0:T(8,128)(2,1)S(1)} %bitcast.9), custom_call_target="tpu_custom_call" | custom-call | tf_op jit(solution)/shard_map/combine/pallas_call | solution.py:193
Async XLA Ops:
  0.0 0.9 %copy-start.1 = (bf16[32,2,8,128]{3,2,1,0:T(8,128)(2,1)S(1)}, bf16[32,2,8,128]{3,2,1,0:T(8,128)(2,1)}, u32[]{:S(2)}) copy-start(bf16[32,2,8,128]{3,2,1,0:T(8,128)(2,1)} %param.11) | copy-start | bytes 393220
  0.9 0.7 copy-start.5
  1.6 0.7 copy-start.6
  31.7 2.5 %copy-start = (bf16[40,1,2,256,128]{4,3,2,1,0:T(8,128)(2,1)S(1)}, bf16[40,1,2,256,128]{4,3,2,1,0:T(8,128)(2,1)}, u32[]{:S(2)}) copy-start(bf16[40,1,2,256,128]{4,3,2,1,0:T(8,128)(2,1)} %param.7) | copy-start | bytes 15728644
  46.1 23.9 %copy-start.2 = (bf16[32,2,8,128]{3,2,1,0:T(8,128)(2,1)S(1)}, bf16[32,2,8,128]{3,2,1,0:T(8,128)(2,1)}, u32[]{:S(2)}) copy-start(bf16[32,2,8,128]{3,2,1,0:T(8,128)(2,1)} %param.11) | copy-start | bytes 393220
  46.1 23.9 %copy-start.3 = (bf16[32,2,1,128]{3,1,2,0:T(2,128)(2,1)S(1)}, bf16[32,2,1,128]{3,1,2,0:T(2,128)(2,1)}, u32[]{:S(2)}) copy-start(bf16[32,2,1,128]{3,1,2,0:T(2,128)(2,1)} %param.12) | copy-start | bytes 49156
  46.1 23.9 %copy-start.4 = (bf16[32,2,1,128]{3,1,2,0:T(2,128)(2,1)S(1)}, bf16[32,2,1,128]{3,1,2,0:T(2,128)(2,1)}, u32[]{:S(2)}) copy-start(bf16[32,2,1,128]{3,1,2,0:T(2,128)(2,1)} %param.13) | copy-start | bytes 49156
  46.1 23.9 %copy-start.7 = (s32[32]{0:T(128)S(1)}, s32[32]{0:T(128)}, u32[]{:S(2)}) copy-start(s32[32]{0:T(128)} %alive_ref.1) | copy-start | bytes 388

commit v2 on v1

v2 whole, which is shorter than its diff:
```python
import jax
import jax.numpy as jnp
from jax import lax
from jax.experimental import pallas as pl
from jax.experimental.pallas import tpu as pltpu
from jax.sharding import PartitionSpec as P

GROUP = 8
PPAGES = 4
POOL_ROW = 40
PAGE = 256
HD = 128
DP = 32
ROWS_DEV = 32
SH = 16
PROMPTS = 16
BRANCH_AT = GROUP * SH
TAIL_AT = BRANCH_AT + SH
TAIL = 8
MSG = TAIL_AT + TAIL
TOTAL_AT = 10
TERM = 20
NEG = -1e30
LN2 = 0.6931471805599453
SCALE = HD ** (-0.5)
TO_LOG2 = SCALE / LN2
BF = jnp.bfloat16
F32 = jnp.float32
CONTRACT_LAST = (((1,), (1,)), ((), ()))
HBM = pl.BlockSpec(memory_space=pltpu.HBM)
VMEM = pl.BlockSpec(memory_space=pltpu.VMEM)
SMEM = pl.BlockSpec(memory_space=pltpu.SMEM)


def params(mib):
    return pltpu.CompilerParams(vmem_limit_bytes=mib * 1024 * 1024)


def pack_kernel(map_hbm, len_hbm, q_hbm, out_ref, map_ref, len_ref, q_ref, held_ref, sems):
    copies = [
        pltpu.make_async_copy(src, dst, sems.at[n])
        for n, (src, dst) in enumerate(((map_hbm, map_ref), (len_hbm, len_ref), (q_hbm, q_ref)))
    ]
    for copy in copies:
        copy.start()
    row = lax.broadcasted_iota(jnp.int32, (TAIL, HD), 0)
    for s in range(DP):
        held_ref[s] = -1
    for copy in copies:
        copy.wait()
    for j in range(PROMPTS):
        page = map_ref[j]
        s = page // POOL_ROW
        held_ref[s] = page - s * POOL_ROW
        g = j // PPAGES
        for i in range(GROUP):
            out_ref[s, i * SH : (i + 1) * SH, :] = q_ref[g * GROUP + i]
    for e in range(ROWS_DEV):
        page = map_ref[PROMPTS + e]
        s = page // POOL_ROW
        out_ref[s, BRANCH_AT:TAIL_AT, :] = q_ref[e]
        numbers = jnp.where(
            row == 0, held_ref[s], jnp.where(row == 1, page - s * POOL_ROW, len_ref[e])
        )
        out_ref[s, TAIL_AT:MSG, :] = numbers.astype(F32).astype(BF)


def attend_kernel(
    in_ref, pool_ref, out_ref, numbers_v, numbers_s, list_s, scores_ref, weights_ref, maxima, totals, sem
):
    lane = lax.broadcasted_iota(jnp.int32, (SH, HD), 1)
    lane8 = lax.broadcasted_iota(jnp.int32, (TAIL, HD), 1)
    token = lax.broadcasted_iota(jnp.int32, (SH, PAGE), 1)
    ones = jnp.ones((PAGE, HD), BF)
    numbers = jnp.zeros((TAIL, HD), F32)
    for b in range(DP):
        numbers = jnp.where(lane8 == b, in_ref[b, TAIL_AT:MSG, :].astype(F32), numbers)
    numbers_v[...] = numbers.astype(jnp.int32)
    copy = pltpu.make_async_copy(numbers_v, numbers_s, sem)
    copy.start()
    maxima[...] = jnp.zeros_like(maxima)
    totals[...] = jnp.zeros_like(totals)
    copy.wait()
    count = jnp.int32(0)
    for b in range(DP):
        list_s[count] = b
        count = count + jnp.where(numbers_s[0, b] >= 0, 1, 0)

    def raw_scores(question, page):
        return lax.dot_general(question, pool_ref[page, 0], CONTRACT_LAST, preferred_element_type=F32)

    def soft(scores):
        highest = jnp.max(scores, axis=1, keepdims=True)
        return highest, jnp.exp2((scores - highest) * TO_LOG2).astype(BF)

    def blend(weights, page):
        values = jnp.concatenate([pool_ref[page, 1], ones], axis=1)
        both = jnp.dot(weights, values, preferred_element_type=F32)
        return both[:, :HD].astype(BF), both[:, HD:]

    for b in range(DP):
        scores = raw_scores(in_ref[b, BRANCH_AT:TAIL_AT, :], numbers_s[1, b])
        scores_ref[b * SH : (b + 1) * SH, :] = jnp.where(token < numbers_s[2, b], scores, NEG)

    def prompt(j, carry):
        b = list_s[j]
        page = numbers_s[0, b]
        highest, weights = soft(raw_scores(in_ref[b, 0:BRANCH_AT, :], page))
        mix, total = blend(weights, page)
        out_ref[b, 0:BRANCH_AT, :] = mix
        top, whole = jnp.zeros((SH, HD), F32), jnp.zeros((SH, HD), F32)
        for i in range(GROUP):
            top = jnp.where(lane == i, highest[i * SH : (i + 1) * SH], top)
            whole = jnp.where(lane == i, total[i * SH : (i + 1) * SH], whole)
        maxima[b] = top
        totals[b] = whole
        return carry

    lax.fori_loop(0, PROMPTS, prompt, 0, unroll=16)

    highest, weights = soft(scores_ref[...])
    weights_ref[...] = weights
    for b in range(DP):
        mix, total = blend(weights_ref[b * SH : (b + 1) * SH, :], numbers_s[1, b])
        out_ref[b, BRANCH_AT:TAIL_AT, :] = mix
        top = jnp.where(lane == GROUP, highest[b * SH : (b + 1) * SH] * SCALE, maxima[b] * SCALE)
        whole = jnp.where(lane == GROUP, total, totals[b])
        both = top + pltpu.roll(whole, TOTAL_AT, 1)
        both = both[0:TAIL] + pltpu.roll(both[TAIL:SH], HD // 2, 1)
        first = both.astype(BF).astype(F32)
        rest = both - first
        second = rest.astype(BF).astype(F32)
        third = rest - second
        tail = first + pltpu.roll(second, TERM, 1) + pltpu.roll(third, 2 * TERM, 1)
        out_ref[b, TAIL_AT:MSG, :] = tail.astype(BF)


def combine_kernel(
    map_ref, alive_ref, in_ref, q_ref, nk_ref, nv_ref, out_ref, fresh_ref, maxima, totals
):
    lane = lax.broadcasted_iota(jnp.int32, (SH, HD), 1)
    question = q_ref[...].reshape(ROWS_DEV * SH, HD)
    scores = lax.dot_general(question, nk_ref[...], CONTRACT_LAST, preferred_element_type=F32)
    at = lax.broadcasted_iota(jnp.int32, scores.shape, 0)
    new = lax.broadcasted_iota(jnp.int32, scores.shape, 1)
    usable = (at // SH == new // 2) & (new % 2 <= (at % SH) // (SH // 2))
    scores = jnp.where(usable, scores, NEG)
    fresh_top = jnp.max(scores, axis=1, keepdims=True)
    weights = jnp.where(usable, jnp.exp2((scores - fresh_top) * TO_LOG2), 0.0).astype(BF)
    fresh_total = jnp.sum(weights.astype(F32), axis=1, keepdims=True)
    mix = jnp.dot(weights, nv_ref[...], preferred_element_type=F32)
    fresh_ref[...] = mix.reshape(ROWS_DEV, SH, HD)
    fresh_top = fresh_top * SCALE

    for s in range(DP):
        tail = in_ref[s, TAIL_AT:MSG, :].astype(F32)
        tail = tail + pltpu.roll(tail, HD - TERM, 1) + pltpu.roll(tail, HD - 2 * TERM, 1)
        both = jnp.concatenate([tail, pltpu.roll(tail, HD // 2, 1)], axis=0)
        maxima[s] = both
        totals[s] = pltpu.roll(both, HD - TOTAL_AT, 1)

    for g in range(ROWS_DEV // GROUP):
        holders = [map_ref[g * PPAGES + k] // POOL_ROW for k in range(PPAGES)]
        tops = [maxima[s] for s in holders]
        wholes = [totals[s] for s in holders]
        own, own_total, fresh, new_total = (jnp.zeros((SH, HD), F32) for _ in range(4))
        homes = []
        for i in range(GROUP):
            row = g * GROUP + i
            s = map_ref[PROMPTS + row] // POOL_ROW
            homes.append(s)
            own = jnp.where(lane == i, maxima[s][:, GROUP : GROUP + 1], own)
            own_total = jnp.where(lane == i, totals[s][:, GROUP : GROUP + 1], own_total)
            fresh = jnp.where(lane == i, fresh_top[row * SH : (row + 1) * SH], fresh)
            new_total = jnp.where(lane == i, fresh_total[row * SH : (row + 1) * SH], new_total)
        tops = tops + [own, fresh]
        wholes = wholes + [own_total, new_total]
        peak = tops[0]
        for top in tops[1:]:
            peak = jnp.maximum(peak, top)
        shares = [jnp.exp(top - peak) for top in tops]
        whole = shares[0] * wholes[0]
        for share, part in zip(shares[1:], wholes[1:]):
            whole = whole + share * part
        shares = [share / whole for share in shares]
        for i in range(GROUP):
            row = g * GROUP + i
            parts = [in_ref[s, i * SH : (i + 1) * SH, :].astype(F32) for s in holders]
            parts.append(in_ref[homes[i], BRANCH_AT:TAIL_AT, :].astype(F32))
            parts.append(fresh_ref[row])
            result = shares[0][:, i : i + 1] * parts[0]
            for share, part in zip(shares[1:], parts[1:]):
                result = result + share[:, i : i + 1] * part
            out_ref[row] = (result * alive_ref[row].astype(F32)).astype(BF)


def pack(page_map, branch_len, question):
    return pl.pallas_call(
        pack_kernel,
        out_shape=jax.ShapeDtypeStruct((DP, MSG, HD), BF),
        in_specs=[HBM, HBM, HBM],
        out_specs=VMEM,
        scratch_shapes=[
            pltpu.SMEM((ROWS_DEV + PROMPTS,), jnp.int32),
            pltpu.SMEM((ROWS_DEV,), jnp.int32),
            pltpu.VMEM((ROWS_DEV, SH, HD), BF),
            pltpu.SMEM((DP,), jnp.int32),
            pltpu.SemaphoreType.DMA((3,)),
        ],
        compiler_params=params(60),
        name="pack",
    )(page_map, branch_len, question)


def attend(asked, pages):
    return pl.pallas_call(
        attend_kernel,
        out_shape=jax.ShapeDtypeStruct((DP, MSG, HD), BF),
        in_specs=[VMEM, VMEM],
        out_specs=VMEM,
        scratch_shapes=[
            pltpu.VMEM((TAIL, HD), jnp.int32),
            pltpu.SMEM((TAIL, HD), jnp.int32),
            pltpu.SMEM((DP + 8,), jnp.int32),
            pltpu.VMEM((DP * SH, PAGE), F32),
            pltpu.VMEM((DP * SH, PAGE), BF),
            pltpu.VMEM((DP, SH, HD), F32),
            pltpu.VMEM((DP, SH, HD), F32),
            pltpu.SemaphoreType.DMA,
        ],
        compiler_params=params(20),
        name="attend",
    )(asked, pages)


def combine(page_map, alive, incoming, question, new_keys, new_values):
    return pl.pallas_call(
        combine_kernel,
        out_shape=jax.ShapeDtypeStruct((ROWS_DEV, SH, HD), BF),
        in_specs=[SMEM, SMEM, VMEM, VMEM, VMEM, VMEM],
        out_specs=VMEM,
        scratch_shapes=[pltpu.VMEM((ROWS_DEV, SH, HD), F32)] + [pltpu.VMEM((DP, SH, HD), F32)] * 2,
        compiler_params=params(20),
        name="combine",
    )(page_map, alive, incoming, question, new_keys, new_values)


def exchange(message):
    return lax.all_to_all(message, "dp", split_axis=0, concat_axis=0, tiled=True)


def shards(pool, page_map, branch_len, alive, queries, new_keys, new_values):
    question = queries.reshape(ROWS_DEV, SH, HD)
    asked = exchange(pack(page_map, branch_len, question))
    incoming = exchange(attend(asked, pool.reshape(POOL_ROW, 2, PAGE, HD)))
    new_keys = new_keys.reshape(ROWS_DEV * 2, HD)
    new_values = new_values.reshape(ROWS_DEV * 2, HD)
    attended = combine(page_map, alive, incoming, question, new_keys, new_values)
    return attended.reshape(queries.shape)


def solution(mesh):
    return jax.shard_map(
        shards,
        mesh=mesh,
        in_specs=(
            P("dp", "tensor", None, None, None),
            P("dp"),
            P("dp"),
            P("dp"),
            P("dp", None, "tensor", None),
            P("dp", None, "tensor", None),
            P("dp", None, "tensor", None),
        ),
        out_specs=P("dp", None, "tensor", None),
        check_vma=False,
    )
```

time: 74.2 us -> 62.8 us (0.85)
  Pallas kernels: 16.8 us -> 8.57 us
  local copies, waits for them, and re-layouts: 4.72 us -> 2.52 us
  blocking collectives: 52.4 us -> 51.4 us
    pallas_call x3, Pallas kernels: 16.8 us -> 8.57 us  [the longest x1 3.38 us: combine(): pl.pallas_call(combine_kernel, out_shape=jax.ShapeDtypeStruct((ROWS_DEV,...]
    unnamed x16 -> x12, local copies, waits for them, and re-layouts: 4.72 us -> 2.52 us
    all_to_all x2, blocking collectives: 52.4 us -> 51.4 us  [exchange(): lax.all_to_all(message, 'dp', split_axis=0, concat_axis=0, tiled=True)]
where the time goes in v2:
time: 62.8 us; the launch traced here: 62.5 us
  blocking collectives  51.4 us (82%)
  Pallas kernels  8.57 us (14%)
  local copies, waits for them, and re-layouts  2.52 us (4%)
    all_to_all x2, blocking collectives, exchange(): lax.all_to_all(message, 'dp', split_axis=0, concat_axis=0, tiled=True)  51.4 us
    pallas_call x1, Pallas kernels, combine(): pl.pallas_call(combine_kernel, out_shape=jax.ShapeDtypeStruct((ROWS_DEV,...  3.38 us
    pallas_call x1, Pallas kernels, attend(): pl.pallas_call(attend_kernel, out_shape=jax.ShapeDtypeStruct((DP, MSG, HD...  2.89 us
    unnamed x12, local copies, waits for them, and re-layouts  2.52 us
    pallas_call x1, Pallas kernels, pack(): pl.pallas_call(pack_kernel, out_shape=jax.ShapeDtypeStruct((DP, MSG, HD),...  2.3 us

profile of v2, /device:TPU:1, one launch (start us, length us, event | category | flops | bytes accessed | tf_op | source)
XLA Modules:
  0.0 62.5 jit_solution(13743789151777323007)
XLA Ops:
  0.0 2.3 %pack.1 = bf16[32,152,128]{2,1,0:T(8,128)(2,1)} custom-call(s32[48]{0:T(128)} %map_ref.1, s32[32]{0:T(128)} %len_hbm.1, bf16[32,16,128]{2,1,0:T(8,128)(2,1)} %bitcast.6), custom_call_target="tpu_custom_call" | custom-call | tf_op jit(solution)/shard_map/pack/pallas_call | solution.py:198
  2.3 28.1 %all_to_all.10.in_ref = bf16[32,152,128]{2,1,0:T(8,128)(2,1)S(1)} all-to-all(bf16[32,152,128]{2,1,0:T(8,128)(2,1)} %pack.1), channel_id=1, replica_groups=mesh['dp'=32,'tensor'=8] {'dp'}, dimensions={0} | all-to-all | bytes 2490368 | tf_op jit(solution)/shard_map/all_to_all | solution.py:249
  30.4 0.0 copy-start
  30.4 2.5 %copy-done = bf16[40,1,2,256,128]{4,3,2,1,0:T(8,128)(2,1)S(1)} copy-done((bf16[40,1,2,256,128]{4,3,2,1,0:T(8,128)(2,1)S(1)}, bf16[40,1,2,256,128]{4,3,2,1,0:T(8,128)(2,1)}, u32[]{:S(2)}) %copy-start) | copy-done | bytes 5242904
  32.9 2.9 %attend.1 = bf16[32,152,128]{2,1,0:T(8,128)(2,1)S(1)} custom-call(bf16[32,152,128]{2,1,0:T(8,128)(2,1)S(1)} %all_to_all.10.in_ref, bf16[40,2,256,128]{3,2,1,0:T(8,128)(2,1)S(1)} %bitcast.5), custom_call_target="tpu_custom_call" | custom-call | tf_op jit(solution)/shard_map/attend/pallas_call | solution.py:216
  35.8 0.0 copy-start.1
  35.8 0.0 copy-start.2
  35.9 0.0 copy-start.3
  35.9 0.0 copy-start.4
  35.9 0.0 copy-start.5
  35.9 23.2 %all_to_all.11.in_ref = bf16[32,152,128]{2,1,0:T(8,128)(2,1)S(1)} all-to-all(bf16[32,152,128]{2,1,0:T(8,128)(2,1)S(1)} %attend.1), channel_id=1, replica_groups=mesh['dp'=32,'tensor'=8] {'dp'}, dimensions={0} | all-to-all | bytes 2490368 | tf_op jit(solution)/shard_map/all_to_all | solution.py:249
  59.1 0.0 copy-done.1
  59.1 0.0 copy-done.2
  59.1 0.0 copy-done.3
  59.1 0.0 copy-done.4
  59.1 0.0 copy-done.5
  59.2 3.4 %combine.1 = bf16[32,16,128]{2,1,0:T(8,128)(2,1)} custom-call(s32[48]{0:T(128)S(1)} %copy-done.4, s32[32]{0:T(128)S(1)} %copy-done.5, bf16[32,152,128]{2,1,0:T(8,128)(2,1)S(1)} %all_to_all.11.in_ref, bf16[32,16,128]{2,1,0:T(8,128)(2,1)S(1)} %bitcast.7, bf16[64,128]{1,0:T(8,128)(2,1)S(1)} %bitcast.8, bf16[64,128]{1,0:T(8,128)(2,1)S(1)} %bitcast.9), custom_call_target="tpu_custom_call" | custom-call | tf_op jit(solution)/shard_map/combine/pallas_call | solution.py:237
Async XLA Ops:
  30.4 2.5 %copy-start = (bf16[40,1,2,256,128]{4,3,2,1,0:T(8,128)(2,1)S(1)}, bf16[40,1,2,256,128]{4,3,2,1,0:T(8,128)(2,1)}, u32[]{:S(2)}) copy-start(bf16[40,1,2,256,128]{4,3,2,1,0:T(8,128)(2,1)} %param.7) | copy-start | bytes 15728644
  35.8 23.3 %copy-start.1 = (bf16[32,2,8,128]{3,2,1,0:T(8,128)(2,1)S(1)}, bf16[32,2,8,128]{3,2,1,0:T(8,128)(2,1)}, u32[]{:S(2)}) copy-start(bf16[32,2,8,128]{3,2,1,0:T(8,128)(2,1)} %param.11) | copy-start | bytes 393220
  35.8 23.3 %copy-start.2 = (bf16[32,2,1,128]{3,1,2,0:T(2,128)(2,1)S(1)}, bf16[32,2,1,128]{3,1,2,0:T(2,128)(2,1)}, u32[]{:S(2)}) copy-start(bf16[32,2,1,128]{3,1,2,0:T(2,128)(2,1)} %param.12) | copy-start | bytes 49156
  35.9 23.3 %copy-start.3 = (bf16[32,2,1,128]{3,1,2,0:T(2,128)(2,1)S(1)}, bf16[32,2,1,128]{3,1,2,0:T(2,128)(2,1)}, u32[]{:S(2)}) copy-start(bf16[32,2,1,128]{3,1,2,0:T(2,128)(2,1)} %param.13) | copy-start | bytes 49156
  35.9 23.3 %copy-start.4 = (s32[48]{0:T(128)S(1)}, s32[48]{0:T(128)}, u32[]{:S(2)}) copy-start(s32[48]{0:T(128)} %map_ref.1) | copy-start | bytes 580
  35.9 23.3 %copy-start.5 = (s32[32]{0:T(128)S(1)}, s32[32]{0:T(128)}, u32[]{:S(2)}) copy-start(s32[32]{0:T(128)} %alive_ref.1) | copy-start | bytes 388

commit v3 on v2

--- a/solution.py
+++ b/solution.py
@@ -17,6 +17,8 @@
 BRANCH_AT = GROUP * SH
 TAIL_AT = BRANCH_AT + SH
 TAIL = 8
+LENGTHS_AT = PROMPTS + ROWS_DEV
+ALIVE_AT = LENGTHS_AT + ROWS_DEV
 MSG = TAIL_AT + TAIL
 TOTAL_AT = 10
 TERM = 20
@@ -27,7 +29,6 @@
 BF = jnp.bfloat16
 F32 = jnp.float32
 CONTRACT_LAST = (((1,), (1,)), ((), ()))
-HBM = pl.BlockSpec(memory_space=pltpu.HBM)
 VMEM = pl.BlockSpec(memory_space=pltpu.VMEM)
 SMEM = pl.BlockSpec(memory_space=pltpu.SMEM)
 
@@ -36,31 +37,23 @@
     return pltpu.CompilerParams(vmem_limit_bytes=mib * 1024 * 1024)
 
 
-def pack_kernel(map_hbm, len_hbm, q_hbm, out_ref, map_ref, len_ref, q_ref, held_ref, sems):
-    copies = [
-        pltpu.make_async_copy(src, dst, sems.at[n])
-        for n, (src, dst) in enumerate(((map_hbm, map_ref), (len_hbm, len_ref), (q_hbm, q_ref)))
-    ]
-    for copy in copies:
-        copy.start()
+def pack_kernel(num_ref, q_ref, out_ref, held_ref):
     row = lax.broadcasted_iota(jnp.int32, (TAIL, HD), 0)
     for s in range(DP):
         held_ref[s] = -1
-    for copy in copies:
-        copy.wait()
     for j in range(PROMPTS):
-        page = map_ref[j]
+        page = num_ref[j]
         s = page // POOL_ROW
         held_ref[s] = page - s * POOL_ROW
         g = j // PPAGES
         for i in range(GROUP):
             out_ref[s, i * SH : (i + 1) * SH, :] = q_ref[g * GROUP + i]
     for e in range(ROWS_DEV):
-        page = map_ref[PROMPTS + e]
+        page = num_ref[PROMPTS + e]
         s = page // POOL_ROW
         out_ref[s, BRANCH_AT:TAIL_AT, :] = q_ref[e]
         numbers = jnp.where(
-            row == 0, held_ref[s], jnp.where(row == 1, page - s * POOL_ROW, len_ref[e])
+            row == 0, held_ref[s], jnp.where(row == 1, page - s * POOL_ROW, num_ref[LENGTHS_AT + e])
         )
         out_ref[s, TAIL_AT:MSG, :] = numbers.astype(F32).astype(BF)
 
@@ -136,7 +129,7 @@
 
 
 def combine_kernel(
-    map_ref, alive_ref, in_ref, q_ref, nk_ref, nv_ref, out_ref, fresh_ref, maxima, totals
+    num_ref, in_ref, q_ref, nk_ref, nv_ref, out_ref, fresh_ref, maxima, totals
 ):
     lane = lax.broadcasted_iota(jnp.int32, (SH, HD), 1)
     question = q_ref[...].reshape(ROWS_DEV * SH, HD)
@@ -160,14 +153,14 @@
         totals[s] = pltpu.roll(both, HD - TOTAL_AT, 1)
 
     for g in range(ROWS_DEV // GROUP):
-        holders = [map_ref[g * PPAGES + k] // POOL_ROW for k in range(PPAGES)]
+        holders = [num_ref[g * PPAGES + k] // POOL_ROW for k in range(PPAGES)]
         tops = [maxima[s] for s in holders]
         wholes = [totals[s] for s in holders]
         own, own_total, fresh, new_total = (jnp.zeros((SH, HD), F32) for _ in range(4))
         homes = []
         for i in range(GROUP):
             row = g * GROUP + i
-            s = map_ref[PROMPTS + row] // POOL_ROW
+            s = num_ref[PROMPTS + row] // POOL_ROW
             homes.append(s)
             own = jnp.where(lane == i, maxima[s][:, GROUP : GROUP + 1], own)
             own_total = jnp.where(lane == i, totals[s][:, GROUP : GROUP + 1], own_total)
@@ -191,25 +184,20 @@
             result = shares[0][:, i : i + 1] * parts[0]
             for share, part in zip(shares[1:], parts[1:]):
                 result = result + share[:, i : i + 1] * part
-            out_ref[row] = (result * alive_ref[row].astype(F32)).astype(BF)
-
-
-def pack(page_map, branch_len, question):
+            out_ref[row] = (result * num_ref[ALIVE_AT + row].astype(F32)).astype(BF)
+
+
+def pack(integers, question):
     return pl.pallas_call(
         pack_kernel,
         out_shape=jax.ShapeDtypeStruct((DP, MSG, HD), BF),
-        in_specs=[HBM, HBM, HBM],
+        in_specs=[SMEM, VMEM],
         out_specs=VMEM,
-        scratch_shapes=[
-            pltpu.SMEM((ROWS_DEV + PROMPTS,), jnp.int32),
-            pltpu.SMEM((ROWS_DEV,), jnp.int32),
-            pltpu.VMEM((ROWS_DEV, SH, HD), BF),
-            pltpu.SMEM((DP,), jnp.int32),
-            pltpu.SemaphoreType.DMA((3,)),
-        ],
-        compiler_params=params(60),
+        scratch_shapes=[pltpu.SMEM((DP,), jnp.int32)],
+        compiler_params=params(8),
+        cost_estimate=pl.CostEstimate(flops=10**11, bytes_accessed=10**8, transcendentals=0),
         name="pack",
-    )(page_map, branch_len, question)
+    )(integers, question)
 
 
 def attend(asked, pages):
@@ -233,16 +221,16 @@
     )(asked, pages)
 
 
-def combine(page_map, alive, incoming, question, new_keys, new_values):
+def combine(integers, incoming, question, new_keys, new_values):
     return pl.pallas_call(
         combine_kernel,
         out_shape=jax.ShapeDtypeStruct((ROWS_DEV, SH, HD), BF),
-        in_specs=[SMEM, SMEM, VMEM, VMEM, VMEM, VMEM],
+        in_specs=[SMEM, VMEM, VMEM, VMEM, VMEM],
         out_specs=VMEM,
         scratch_shapes=[pltpu.VMEM((ROWS_DEV, SH, HD), F32)] + [pltpu.VMEM((DP, SH, HD), F32)] * 2,
         compiler_params=params(20),
         name="combine",
-    )(page_map, alive, incoming, question, new_keys, new_values)
+    )(integers, incoming, question, new_keys, new_values)
 
 
 def exchange(message):
@@ -251,11 +239,12 @@
 
 def shards(pool, page_map, branch_len, alive, queries, new_keys, new_values):
     question = queries.reshape(ROWS_DEV, SH, HD)
-    asked = exchange(pack(page_map, branch_len, question))
+    integers = jnp.concatenate([page_map, branch_len, alive])
+    asked = exchange(pack(integers, question))
     incoming = exchange(attend(asked, pool.reshape(POOL_ROW, 2, PAGE, HD)))
     new_keys = new_keys.reshape(ROWS_DEV * 2, HD)
     new_values = new_values.reshape(ROWS_DEV * 2, HD)
-    attended = combine(page_map, alive, incoming, question, new_keys, new_values)
+    attended = combine(integers, incoming, question, new_keys, new_values)
     return attended.reshape(queries.shape)
 
 

time: 62.8 us -> 60.3 us (0.960)
  Pallas kernels: 8.57 us -> 7.12 us
  local copies, waits for them, and re-layouts: 2.52 us -> 1.08 us
  other arithmetic: 0 us -> 0.76 us
    unnamed x12, local copies, waits for them, and re-layouts: 2.52 us -> 1.08 us
    pallas_call x1, Pallas kernels: 2.3 us -> 0.87 us  [pack(): pl.pallas_call(pack_kernel, out_shape=jax.ShapeDtypeStruct((DP, MSG, HD),...]
    concatenate x0 -> x1, other arithmetic: none -> 0.76 us  [shards(): integers = jnp.concatenate([page_map, branch_len, alive])]
where the time goes in v3:
time: 60.3 us; the launch traced here: 60.2 us
  blocking collectives  51.2 us (85%)
  Pallas kernels  7.12 us (12%)
  local copies, waits for them, and re-layouts  1.08 us (2%)
  other arithmetic  0.76 us (1%)
    all_to_all x2, blocking collectives, exchange(): lax.all_to_all(message, 'dp', split_axis=0, concat_axis=0, tiled=True)  51.2 us
    pallas_call x1, Pallas kernels, combine(): pl.pallas_call(combine_kernel, out_shape=jax.ShapeDtypeStruct((ROWS_DEV,...  3.39 us
    pallas_call x1, Pallas kernels, attend(): pl.pallas_call(attend_kernel, out_shape=jax.ShapeDtypeStruct((DP, MSG, HD...  2.86 us

profile of v3, /device:TPU:1, one launch (start us, length us, event | category | flops | bytes accessed | tf_op | source)
XLA Modules:
  0.0 60.2 jit_solution(17911548337245884596)
XLA Ops:
  0.0 0.8 %pad_add_fusion.num_ref = s32[112]{0:T(128)S(1)} fusion(s32[32]{0:T(128)} %param.10, s32[32]{0:T(128)} %param.9, s32[48]{0:T(128)} %param.8), kind=kLoop, calls=%fused_computation | loop fusion | flops 224 | bytes 896 | tf_op jit(solution)/shard_map/concatenate | solution.py:242
  0.8 0.0 slice-start
  0.8 0.0 copy-start
  0.8 1.1 %copy-done = bf16[32,2,8,128]{3,2,1,0:T(8,128)(2,1)S(1)} copy-done((bf16[32,2,8,128]{3,2,1,0:T(8,128)(2,1)S(1)}, bf16[32,2,8,128]{3,2,1,0:T(8,128)(2,1)}, u32[]{:S(2)}) %copy-start) | copy-done | bytes 131096
  1.8 0.0 slice-start.1
  1.8 0.9 %pack.1 = bf16[32,152,128]{2,1,0:T(8,128)(2,1)S(1)} custom-call(s32[112]{0:T(128)S(1)} %pad_add_fusion.num_ref, bf16[32,16,128]{2,1,0:T(8,128)(2,1)S(1)} %bitcast.8), custom_call_target="tpu_custom_call" | custom-call | flops 99999997952 | bytes 100000000 | tf_op jit(solution)/shard_map/pack/pallas_call | solution.py:191
  2.7 27.9 %all_to_all.10.in_ref = bf16[32,152,128]{2,1,0:T(8,128)(2,1)S(1)} all-to-all(bf16[32,152,128]{2,1,0:T(8,128)(2,1)S(1)} %pack.1), channel_id=1, replica_groups=mesh['dp'=32,'tensor'=8] {'dp'}, dimensions={0} | all-to-all | bytes 2490368 | tf_op jit(solution)/shard_map/all_to_all | solution.py:237
  30.6 0.0 slice-done
  30.6 0.0 slice-done.1
  30.6 2.9 %attend.1 = bf16[32,152,128]{2,1,0:T(8,128)(2,1)S(1)} custom-call(bf16[32,152,128]{2,1,0:T(8,128)(2,1)S(1)} %all_to_all.10.in_ref, bf16[40,2,256,128]{3,2,1,0:T(8,128)(2,1)S(1)} %bitcast.7), custom_call_target="tpu_custom_call" | custom-call | tf_op jit(solution)/shard_map/attend/pallas_call | solution.py:204
  33.5 0.0 copy-start.1
  33.5 0.0 copy-start.2
  33.5 0.0 copy-start.3
  33.5 23.2 %all_to_all.11.in_ref = bf16[32,152,128]{2,1,0:T(8,128)(2,1)S(1)} all-to-all(bf16[32,152,128]{2,1,0:T(8,128)(2,1)S(1)} %attend.1), channel_id=1, replica_groups=mesh['dp'=32,'tensor'=8] {'dp'}, dimensions={0} | all-to-all | bytes 2490368 | tf_op jit(solution)/shard_map/all_to_all | solution.py:237
  56.8 0.0 copy-done.1
  56.8 0.0 copy-done.2
  56.8 0.0 copy-done.3
  56.8 3.4 %combine.1 = bf16[32,16,128]{2,1,0:T(8,128)(2,1)} custom-call(s32[112]{0:T(128)S(1)} %pad_add_fusion.num_ref, bf16[32,152,128]{2,1,0:T(8,128)(2,1)S(1)} %all_to_all.11.in_ref, bf16[32,16,128]{2,1,0:T(8,128)(2,1)S(1)} %bitcast.9, bf16[64,128]{1,0:T(8,128)(2,1)S(1)} %bitcast.10, bf16[64,128]{1,0:T(8,128)(2,1)S(1)} %bitcast.11), custom_call_target="tpu_custom_call" | custom-call | tf_op jit(solution)/shard_map/combine/pallas_call | solution.py:225
  (1 shorter events, 0.0 us)
Async XLA Ops:
  0.8 29.9 %slice-start = ((s8[5242880]{0:T(1024)(128)(4,1)}), s8[4194304]{0:T(1024)(128)(4,1)S(1)}, s32[]{:S(2)}) async-start(s8[5242880]{0:T(1024)(128)(4,1)} %bitcast.5), calls=%async_computation.2 | async-start | bytes 8388608
  0.8 1.1 %copy-start = (bf16[32,2,8,128]{3,2,1,0:T(8,128)(2,1)S(1)}, bf16[32,2,8,128]{3,2,1,0:T(8,128)(2,1)}, u32[]{:S(2)}) copy-start(bf16[32,2,8,128]{3,2,1,0:T(8,128)(2,1)} %param.11) | copy-start | bytes 393220
  1.8 28.8 %slice-start.1 = ((s8[5242880]{0:T(1024)(128)(4,1)}), s8[1048576]{0:T(1024)(128)(4,1)S(1)}, s32[]{:S(2)}) async-start(s8[5242880]{0:T(1024)(128)(4,1)} %bitcast.5), calls=%async_computation.3 | async-start | bytes 2097152
  33.5 23.3 %copy-start.1 = (bf16[32,2,8,128]{3,2,1,0:T(8,128)(2,1)S(1)}, bf16[32,2,8,128]{3,2,1,0:T(8,128)(2,1)}, u32[]{:S(2)}) copy-start(bf16[32,2,8,128]{3,2,1,0:T(8,128)(2,1)} %param.11) | copy-start | bytes 393220
  33.5 23.3 %copy-start.2 = (bf16[32,2,1,128]{3,1,2,0:T(2,128)(2,1)S(1)}, bf16[32,2,1,128]{3,1,2,0:T(2,128)(2,1)}, u32[]{:S(2)}) copy-start(bf16[32,2,1,128]{3,1,2,0:T(2,128)(2,1)} %param.12) | copy-start | bytes 49156
  33.5 23.3 %copy-start.3 = (bf16[32,2,1,128]{3,1,2,0:T(2,128)(2,1)S(1)}, bf16[32,2,1,128]{3,1,2,0:T(2,128)(2,1)}, u32[]{:S(2)}) copy-start(bf16[32,2,1,128]{3,1,2,0:T(2,128)(2,1)} %param.13) | copy-start | bytes 49156

commit v4 on v2

v4 whole, which is shorter than its diff:
```python
import jax
import jax.numpy as jnp
from jax import lax
from jax.experimental import pallas as pl
from jax.experimental.pallas import tpu as pltpu
from jax.sharding import PartitionSpec as P

GROUP = 8
PPAGES = 4
POOL_ROW = 40
PAGE = 256
HD = 128
DP = 32
ROWS_DEV = 32
SH = 16
PROMPTS = 16
BRANCH_AT = GROUP * SH
TAIL_AT = BRANCH_AT + SH
TAIL = 8
MSG = TAIL_AT + TAIL
TOTAL_AT = 32
TERM = 10
NEG = -1e30
LN2 = 0.6931471805599453
SCALE = HD ** (-0.5)
TO_LOG2 = SCALE / LN2
BF = jnp.bfloat16
F32 = jnp.float32
CONTRACT_LAST = (((1,), (1,)), ((), ()))
VMEM = pl.BlockSpec(memory_space=pltpu.VMEM)
SMEM = pl.BlockSpec(memory_space=pltpu.SMEM)


def params(mib):
    return pltpu.CompilerParams(vmem_limit_bytes=mib * 1024 * 1024)


def blank_kernel(held_ref):
    held_ref[...] = jnp.full(held_ref.shape, -1, jnp.int32)


def pack_kernel(map_ref, len_ref, blank_ref, q_ref, out_ref, held_ref):
    row = lax.broadcasted_iota(jnp.int32, (TAIL, HD), 0)
    for s in range(DP):
        held_ref[s] = blank_ref[0, s]
    for j in range(PROMPTS):
        page = map_ref[j]
        s = page // POOL_ROW
        held_ref[s] = page - s * POOL_ROW
        g = j // PPAGES
        for i in range(GROUP):
            out_ref[s, i * SH : (i + 1) * SH, :] = q_ref[g * GROUP + i]
    for e in range(ROWS_DEV):
        page = map_ref[PROMPTS + e]
        s = page // POOL_ROW
        out_ref[s, BRANCH_AT:TAIL_AT, :] = q_ref[e]
        numbers = jnp.where(
            row == 0, held_ref[s], jnp.where(row == 1, page - s * POOL_ROW, len_ref[e])
        )
        out_ref[s, TAIL_AT:MSG, :] = numbers.astype(F32).astype(BF)


def attend_kernel(
    in_ref, pool_ref, out_ref, numbers_s, list_s, scores_ref, weights_ref, maxima, totals
):
    lane = lax.broadcasted_iota(jnp.int32, (SH, HD), 1)
    token = lax.broadcasted_iota(jnp.int32, (SH, PAGE), 1)
    ones = jnp.ones((PAGE, HD), BF)
    count = jnp.int32(0)
    for b in range(DP):
        numbers = in_ref[b, TAIL_AT:MSG, :].astype(F32).astype(jnp.int32)
        list_s[count] = b
        count = count + jnp.where(numbers[0, 0] >= 0, 1, 0)
        for k in range(3):
            numbers_s[k, b] = numbers[k, 0]
    maxima[...] = jnp.zeros_like(maxima)
    totals[...] = jnp.zeros_like(totals)

    def raw_scores(question, page):
        return lax.dot_general(question, pool_ref[page, 0], CONTRACT_LAST, preferred_element_type=F32)

    def soft(scores):
        highest = jnp.max(scores, axis=1, keepdims=True)
        return highest, jnp.exp2((scores - highest) * TO_LOG2).astype(BF)

    def blend(weights, page):
        values = jnp.concatenate([pool_ref[page, 1], ones], axis=1)
        both = jnp.dot(weights, values, preferred_element_type=F32)
        return both[:, :HD].astype(BF), both[:, HD:]

    for b in range(DP):
        scores = raw_scores(in_ref[b, BRANCH_AT:TAIL_AT, :], numbers_s[1, b])
        scores_ref[b * SH : (b + 1) * SH, :] = jnp.where(token < numbers_s[2, b], scores, NEG)

    def prompt(j, carry):
        b = list_s[j]
        page = numbers_s[0, b]
        highest, weights = soft(raw_scores(in_ref[b, 0:BRANCH_AT, :], page))
        mix, total = blend(weights, page)
        out_ref[b, 0:BRANCH_AT, :] = mix
        top, whole = jnp.zeros((SH, HD), F32), jnp.zeros((SH, HD), F32)
        for i in range(GROUP):
            top = jnp.where(lane == i, highest[i * SH : (i + 1) * SH], top)
            whole = jnp.where(lane == i, total[i * SH : (i + 1) * SH], whole)
        maxima[b] = top
        totals[b] = whole
        return carry

    lax.fori_loop(0, PROMPTS, prompt, 0, unroll=16)

    highest, weights = soft(scores_ref[...])
    weights_ref[...] = weights
    total = jnp.sum(weights.astype(F32), axis=1, keepdims=True)
    for b in range(DP):
        values = pool_ref[numbers_s[1, b], 1]
        mix = jnp.dot(weights_ref[b * SH : (b + 1) * SH, :], values, preferred_element_type=F32)
        out_ref[b, BRANCH_AT:TAIL_AT, :] = mix.astype(BF)
        top = jnp.where(lane == GROUP, highest[b * SH : (b + 1) * SH] * SCALE, maxima[b] * SCALE)
        whole = jnp.where(lane == GROUP, total[b * SH : (b + 1) * SH], totals[b])
        both = top + pltpu.roll(whole, TOTAL_AT, 1)
        both = both[0:TAIL] + pltpu.roll(both[TAIL:SH], HD // 2, 1)
        first = both.astype(BF).astype(F32)
        rest = both - first
        second = rest.astype(BF).astype(F32)
        third = rest - second
        tail = first + pltpu.roll(second, TERM, 1) + pltpu.roll(third, 2 * TERM, 1)
        out_ref[b, TAIL_AT:MSG, :] = tail.astype(BF)


def combine_kernel(
    map_ref, alive_ref, in_ref, q_ref, nk_ref, nv_ref, out_ref, fresh_ref, numbers_ref
):
    half = SH // 2
    lane = lax.broadcasted_iota(jnp.int32, (half, HD), 1)
    place = lane % TOTAL_AT
    question = q_ref[...].reshape(ROWS_DEV * SH, HD)
    scores = lax.dot_general(question, nk_ref[...], CONTRACT_LAST, preferred_element_type=F32)
    at = lax.broadcasted_iota(jnp.int32, scores.shape, 0)
    new = lax.broadcasted_iota(jnp.int32, scores.shape, 1)
    usable = (at // SH == new // 2) & (new % 2 <= (at % SH) // half)
    scores = jnp.where(usable, scores, NEG)
    top = jnp.max(scores, axis=1, keepdims=True)
    weights = jnp.where(usable, jnp.exp2((scores - top) * TO_LOG2), 0.0).astype(BF)
    total = jnp.sum(weights.astype(F32), axis=1, keepdims=True)
    mix = jnp.dot(weights, nv_ref[...], preferred_element_type=F32)
    fresh_ref[...] = mix.reshape(ROWS_DEV, SH, HD)
    top = top * SCALE

    fresh = jnp.zeros((half, HD), F32)
    for r in range(ROWS_DEV):
        for n, column in enumerate((top, total)):
            for m in range(2):
                piece = column[r * SH + m * half : r * SH + (m + 1) * half]
                fresh = jnp.where(lane == m * HD // 2 + n * TOTAL_AT + r, piece, fresh)

    for s in range(DP):
        tail = in_ref[s, TAIL_AT:MSG, :].astype(F32)
        numbers_ref[s] = tail + pltpu.roll(tail, HD - TERM, 1) + pltpu.roll(tail, HD - 2 * TERM, 1)

    holders = [map_ref[j] // POOL_ROW for j in range(PROMPTS + ROWS_DEV)]
    blocks = []
    for k in range(PPAGES):
        block = numbers_ref[holders[k]]
        for g in range(1, ROWS_DEV // GROUP):
            own = pltpu.roll(numbers_ref[holders[g * PPAGES + k]], g * GROUP, 1)
            block = jnp.where(place // GROUP == g, own, block)
        blocks.append(block)
    block = jnp.zeros((half, HD), F32)
    for r in range(ROWS_DEV):
        own = pltpu.roll(numbers_ref[holders[PROMPTS + r]], (r - GROUP) % HD, 1)
        block = jnp.where(place == r, own, block)
    blocks += [block, fresh]

    peak = blocks[0]
    for block in blocks[1:]:
        peak = jnp.maximum(peak, block)
    shares = [jnp.exp(block - peak) for block in blocks]
    wholes = [share * pltpu.roll(block, HD - TOTAL_AT, 1) for share, block in zip(shares, blocks)]
    whole = wholes[0]
    for part in wholes[1:]:
        whole = whole + part
    shares = [share / whole for share in shares]

    for r in range(ROWS_DEV):
        g, i = r // GROUP, r % GROUP
        parts = [
            in_ref[holders[g * PPAGES + k], i * SH : (i + 1) * SH, :].astype(F32)
            for k in range(PPAGES)
        ]
        parts.append(in_ref[holders[PROMPTS + r], BRANCH_AT:TAIL_AT, :].astype(F32))
        parts.append(fresh_ref[r])
        result = None
        for share, part in zip(shares, parts):
            column = jnp.concatenate(
                [share[:, r : r + 1], share[:, HD // 2 + r : HD // 2 + r + 1]], axis=0
            )
            result = column * part if result is None else result + column * part
        out_ref[r] = (result * alive_ref[r].astype(F32)).astype(BF)


def blank():
    return pl.pallas_call(
        blank_kernel,
        out_shape=jax.ShapeDtypeStruct((1, HD), jnp.int32),
        out_specs=VMEM,
        compiler_params=params(8),
        cost_estimate=pl.CostEstimate(flops=10**11, bytes_accessed=10**8, transcendentals=0),
        name="blank",
    )()


def pack(page_map, branch_len, question):
    return pl.pallas_call(
        pack_kernel,
        out_shape=jax.ShapeDtypeStruct((DP, MSG, HD), BF),
        in_specs=[SMEM, SMEM, SMEM, VMEM],
        out_specs=VMEM,
        scratch_shapes=[pltpu.SMEM((DP,), jnp.int32)],
        compiler_params=params(8),
        cost_estimate=pl.CostEstimate(flops=10**11, bytes_accessed=10**8, transcendentals=0),
        name="pack",
    )(page_map, branch_len, blank(), question)


def attend(asked, pages):
    return pl.pallas_call(
        attend_kernel,
        out_shape=jax.ShapeDtypeStruct((DP, MSG, HD), BF),
        in_specs=[VMEM, VMEM],
        out_specs=VMEM,
        scratch_shapes=[
            pltpu.SMEM((3, DP), jnp.int32),
            pltpu.SMEM((DP + 8,), jnp.int32),
            pltpu.VMEM((DP * SH, PAGE), F32),
            pltpu.VMEM((DP * SH, PAGE), BF),
            pltpu.VMEM((DP, SH, HD), F32),
            pltpu.VMEM((DP, SH, HD), F32),
        ],
        compiler_params=params(20),
        name="attend",
    )(asked, pages)


def combine(page_map, alive, incoming, question, new_keys, new_values):
    return pl.pallas_call(
        combine_kernel,
        out_shape=jax.ShapeDtypeStruct((ROWS_DEV, SH, HD), BF),
        in_specs=[SMEM, SMEM, VMEM, VMEM, VMEM, VMEM],
        out_specs=VMEM,
        scratch_shapes=[pltpu.VMEM((ROWS_DEV, SH, HD), F32), pltpu.VMEM((DP, TAIL, HD), F32)],
        compiler_params=params(20),
        name="combine",
    )(page_map, alive, incoming, question, new_keys, new_values)


def exchange(message):
    return lax.all_to_all(message, "dp", split_axis=0, concat_axis=0, tiled=True)


def shards(pool, page_map, branch_len, alive, queries, new_keys, new_values):
    question = queries.reshape(ROWS_DEV, SH, HD)
    asked = exchange(pack(page_map, branch_len, question))
    incoming = exchange(attend(asked, pool.reshape(POOL_ROW, 2, PAGE, HD)))
    new_keys = new_keys.reshape(ROWS_DEV * 2, HD)
    new_values = new_values.reshape(ROWS_DEV * 2, HD)
    attended = combine(page_map, alive, incoming, question, new_keys, new_values)
    return attended.reshape(queries.shape)


def solution(mesh):
    return jax.shard_map(
        shards,
        mesh=mesh,
        in_specs=(
            P("dp", "tensor", None, None, None),
            P("dp"),
            P("dp"),
            P("dp"),
            P("dp", None, "tensor", None),
            P("dp", None, "tensor", None),
            P("dp", None, "tensor", None),
        ),
        out_specs=P("dp", None, "tensor", None),
        check_vma=False,
    )
```

time: 62.8 us -> 57.5 us (0.916)
  Pallas kernels: 8.57 us -> 5.2 us
  local copies, waits for them, and re-layouts: 2.52 us -> 0.92 us
    unnamed x12 -> x16, local copies, waits for them, and re-layouts: 2.52 us -> 0.92 us
    pallas_call x1, Pallas kernels: 2.3 us -> 0.89 us  [pack(): pl.pallas_call(pack_kernel, out_shape=jax.ShapeDtypeStruct((DP, MSG, HD),...]
    pallas_call x1, Pallas kernels: 2.89 us -> 1.88 us  [attend(): pl.pallas_call(attend_kernel, out_shape=jax.ShapeDtypeStruct((DP, MSG, HD...]
    pallas_call x1, Pallas kernels: 3.38 us -> 2.42 us  [combine(): pl.pallas_call(combine_kernel, out_shape=jax.ShapeDtypeStruct((ROWS_DEV,...]
where the time goes in v4:
time: 57.5 us; the launch traced here: 57.3 us
  blocking collectives  51.2 us (89%)
  Pallas kernels  5.2 us (9%)
  local copies, waits for them, and re-layouts  0.92 us (2%)
    all_to_all x2, blocking collectives, exchange(): lax.all_to_all(message, 'dp', split_axis=0, concat_axis=0, tiled=True)  51.2 us
    pallas_call x1, Pallas kernels, combine(): pl.pallas_call(combine_kernel, out_shape=jax.ShapeDtypeStruct((ROWS_DEV,...  2.42 us
    pallas_call x1, Pallas kernels, attend(): pl.pallas_call(attend_kernel, out_shape=jax.ShapeDtypeStruct((DP, MSG, HD...  1.88 us

profile of v4, /device:TPU:1, one launch (start us, length us, event | category | flops | bytes accessed | tf_op | source)
XLA Modules:
  0.0 57.3 jit_solution(16291232006378467982)
XLA Ops:
  0.0 0.0 copy-start.3
  0.0 0.0 copy-start
  0.0 0.0 copy-start.5
  0.0 0.0 slice-start
  0.0 0.6 %copy-done.3 = s32[48]{0:T(128)S(1)} copy-done((s32[48]{0:T(128)S(1)}, s32[48]{0:T(128)}, u32[]{:S(2)}) %copy-start.3) | copy-done | bytes 216
  0.7 0.3 copy-done
  0.9 0.0 copy-done.5
  0.9 0.0 slice-start.1
  0.9 0.9 %pack.1 = bf16[32,152,128]{2,1,0:T(8,128)(2,1)S(1)} custom-call(s32[48]{0:T(128)S(1)} %copy-done.3, s32[32]{0:T(128)S(1)} %copy-done.5, s32[1,128]{1,0:T(1,128)S(1)} %blank.1.blank_ref, bf16[32,16,128]{2,1,0:T(8,128)(2,1)S(1)} %bitcast.8), custom_call_target="tpu_custom_call" | custom-call | flops 99999997952 | bytes 100000000 | tf_op jit(solution)/shard_map/pack/pallas_call | solution.py:213
  1.8 27.9 %all_to_all.10.in_ref = bf16[32,152,128]{2,1,0:T(8,128)(2,1)S(1)} all-to-all(bf16[32,152,128]{2,1,0:T(8,128)(2,1)S(1)} %pack.1), channel_id=1, replica_groups=mesh['dp'=32,'tensor'=8] {'dp'}, dimensions={0} | all-to-all | bytes 2490368 | tf_op jit(solution)/shard_map/all_to_all | solution.py:257
  29.8 0.0 slice-done
  29.8 0.0 slice-done.1
  29.8 1.9 %attend.1 = bf16[32,152,128]{2,1,0:T(8,128)(2,1)S(1)} custom-call(bf16[32,152,128]{2,1,0:T(8,128)(2,1)S(1)} %all_to_all.10.in_ref, bf16[40,2,256,128]{3,2,1,0:T(8,128)(2,1)S(1)} %bitcast.7), custom_call_target="tpu_custom_call" | custom-call | tf_op jit(solution)/shard_map/attend/pallas_call | solution.py:226
  31.6 0.0 copy-start.1
  31.7 0.0 copy-start.2
  31.7 0.0 copy-start.4
  31.7 23.2 %all_to_all.11.in_ref = bf16[32,152,128]{2,1,0:T(8,128)(2,1)S(1)} all-to-all(bf16[32,152,128]{2,1,0:T(8,128)(2,1)S(1)} %attend.1), channel_id=1, replica_groups=mesh['dp'=32,'tensor'=8] {'dp'}, dimensions={0} | all-to-all | bytes 2490368 | tf_op jit(solution)/shard_map/all_to_all | solution.py:257
  54.9 0.0 copy-done.1
  54.9 0.0 copy-done.2
  54.9 0.0 copy-done.4
  54.9 2.4 %combine.1 = bf16[32,16,128]{2,1,0:T(8,128)(2,1)} custom-call(s32[48]{0:T(128)S(1)} %copy-done.3, s32[32]{0:T(128)S(1)} %copy-done.4, bf16[32,152,128]{2,1,0:T(8,128)(2,1)S(1)} %all_to_all.11.in_ref, bf16[32,16,128]{2,1,0:T(8,128)(2,1)S(1)} %bitcast.9, bf16[64,128]{1,0:T(8,128)(2,1)S(1)} %bitcast.10, bf16[64,128]{1,0:T(8,128)(2,1)S(1)} %bitcast.11), custom_call_target="tpu_custom_call" | custom-call | tf_op jit(solution)/shard_map/combine/pallas_call | solution.py:245
  (2 shorter events, 0.0 us)
Async XLA Ops:
  0.0 0.7 %copy-start.3 = (s32[48]{0:T(128)S(1)}, s32[48]{0:T(128)}, u32[]{:S(2)}) copy-start(s32[48]{0:T(128)} %map_ref.3) | copy-start | bytes 580
  0.0 0.9 %copy-start = (bf16[32,2,8,128]{3,2,1,0:T(8,128)(2,1)S(1)}, bf16[32,2,8,128]{3,2,1,0:T(8,128)(2,1)}, u32[]{:S(2)}) copy-start(bf16[32,2,8,128]{3,2,1,0:T(8,128)(2,1)} %param.11) | copy-start | bytes 393220
  0.0 0.9 %copy-start.5 = (s32[32]{0:T(128)S(1)}, s32[32]{0:T(128)}, u32[]{:S(2)}) copy-start(s32[32]{0:T(128)} %len_ref.1) | copy-start | bytes 388
  0.0 29.7 %slice-start = ((s8[5242880]{0:T(1024)(128)(4,1)}), s8[4194304]{0:T(1024)(128)(4,1)S(1)}, s32[]{:S(2)}) async-start(s8[5242880]{0:T(1024)(128)(4,1)} %bitcast.5), calls=%async_computation.2 | async-start | bytes 8388608
  0.9 28.8 %slice-start.1 = ((s8[5242880]{0:T(1024)(128)(4,1)}), s8[1048576]{0:T(1024)(128)(4,1)S(1)}, s32[]{:S(2)}) async-start(s8[5242880]{0:T(1024)(128)(4,1)} %bitcast.5), calls=%async_computation.3 | async-start | bytes 2097152
  31.6 23.3 %copy-start.1 = (bf16[32,2,1,128]{3,1,2,0:T(2,128)(2,1)S(1)}, bf16[32,2,1,128]{3,1,2,0:T(2,128)(2,1)}, u32[]{:S(2)}) copy-start(bf16[32,2,1,128]{3,1,2,0:T(2,128)(2,1)} %param.12) | copy-start | bytes 49156
  31.7 23.3 %copy-start.2 = (bf16[32,2,1,128]{3,1,2,0:T(2,128)(2,1)S(1)}, bf16[32,2,1,128]{3,1,2,0:T(2,128)(2,1)}, u32[]{:S(2)}) copy-start(bf16[32,2,1,128]{3,1,2,0:T(2,128)(2,1)} %param.13) | copy-start | bytes 49156
  31.7 23.3 %copy-start.4 = (s32[32]{0:T(128)S(1)}, s32[32]{0:T(128)}, u32[]{:S(2)}) copy-start(s32[32]{0:T(128)} %alive_ref.1) | copy-start | bytes 388

commit v5 on v4

--- a/solution.py
+++ b/solution.py
@@ -41,21 +41,22 @@
 
 def pack_kernel(map_ref, len_ref, blank_ref, q_ref, out_ref, held_ref):
     row = lax.broadcasted_iota(jnp.int32, (TAIL, HD), 0)
+    pages, lengths, blank = map_ref[...], len_ref[...], blank_ref[...]
     for s in range(DP):
-        held_ref[s] = blank_ref[0, s]
+        held_ref[s] = blank[0, s]
     for j in range(PROMPTS):
-        page = map_ref[j]
+        page = pages[0, j]
         s = page // POOL_ROW
         held_ref[s] = page - s * POOL_ROW
         g = j // PPAGES
         for i in range(GROUP):
             out_ref[s, i * SH : (i + 1) * SH, :] = q_ref[g * GROUP + i]
     for e in range(ROWS_DEV):
-        page = map_ref[PROMPTS + e]
+        page = pages[0, PROMPTS + e]
         s = page // POOL_ROW
         out_ref[s, BRANCH_AT:TAIL_AT, :] = q_ref[e]
         numbers = jnp.where(
-            row == 0, held_ref[s], jnp.where(row == 1, page - s * POOL_ROW, len_ref[e])
+            row == 0, held_ref[s], jnp.where(row == 1, page - s * POOL_ROW, lengths[0, e])
         )
         out_ref[s, TAIL_AT:MSG, :] = numbers.astype(F32).astype(BF)
 
@@ -157,7 +158,8 @@
         tail = in_ref[s, TAIL_AT:MSG, :].astype(F32)
         numbers_ref[s] = tail + pltpu.roll(tail, HD - TERM, 1) + pltpu.roll(tail, HD - 2 * TERM, 1)
 
-    holders = [map_ref[j] // POOL_ROW for j in range(PROMPTS + ROWS_DEV)]
+    pages, kept = map_ref[...], alive_ref[...]
+    holders = [pages[0, j] // POOL_ROW for j in range(PROMPTS + ROWS_DEV)]
     blocks = []
     for k in range(PPAGES):
         block = numbers_ref[holders[k]]
@@ -195,7 +197,7 @@
                 [share[:, r : r + 1], share[:, HD // 2 + r : HD // 2 + r + 1]], axis=0
             )
             result = column * part if result is None else result + column * part
-        out_ref[r] = (result * alive_ref[r].astype(F32)).astype(BF)
+        out_ref[r] = (result * kept[0, r].astype(F32)).astype(BF)
 
 
 def blank():
@@ -213,7 +215,7 @@
     return pl.pallas_call(
         pack_kernel,
         out_shape=jax.ShapeDtypeStruct((DP, MSG, HD), BF),
-        in_specs=[SMEM, SMEM, SMEM, VMEM],
+        in_specs=[VMEM, VMEM, VMEM, VMEM],
         out_specs=VMEM,
         scratch_shapes=[pltpu.SMEM((DP,), jnp.int32)],
         compiler_params=params(8),
@@ -245,7 +247,7 @@
     return pl.pallas_call(
         combine_kernel,
         out_shape=jax.ShapeDtypeStruct((ROWS_DEV, SH, HD), BF),
-        in_specs=[SMEM, SMEM, VMEM, VMEM, VMEM, VMEM],
+        in_specs=[VMEM, VMEM, VMEM, VMEM, VMEM, VMEM],
         out_specs=VMEM,
         scratch_shapes=[pltpu.VMEM((ROWS_DEV, SH, HD), F32), pltpu.VMEM((DP, TAIL, HD), F32)],
         compiler_params=params(20),
@@ -259,11 +261,11 @@
 
 def shards(pool, page_map, branch_len, alive, queries, new_keys, new_values):
     question = queries.reshape(ROWS_DEV, SH, HD)
-    asked = exchange(pack(page_map, branch_len, question))
+    asked = exchange(pack(page_map.reshape(1, -1), branch_len.reshape(1, -1), question))
     incoming = exchange(attend(asked, pool.reshape(POOL_ROW, 2, PAGE, HD)))
     new_keys = new_keys.reshape(ROWS_DEV * 2, HD)
     new_values = new_values.reshape(ROWS_DEV * 2, HD)
-    attended = combine(page_map, alive, incoming, question, new_keys, new_values)
+    attended = combine(page_map.reshape(1, -1), alive.reshape(1, -1), incoming, question, new_keys, new_values)
     return attended.reshape(queries.shape)
 
 

time: 57.5 us -> 56.9 us (0.990)
  Pallas kernels: 5.2 us -> 4.48 us
where the time goes in v5:
time: 56.9 us; the launch traced here: 56.8 us
  blocking collectives  51.3 us (90%)
  Pallas kernels  4.48 us (8%)
  local copies, waits for them, and re-layouts  0.91 us (2%)
    all_to_all x2, blocking collectives, exchange(): lax.all_to_all(message, 'dp', split_axis=0, concat_axis=0, tiled=True)  51.3 us
    pallas_call x1, Pallas kernels, combine(): pl.pallas_call(combine_kernel, out_shape=jax.ShapeDtypeStruct((ROWS_DEV,...  2.12 us
    pallas_call x1, Pallas kernels, attend(): pl.pallas_call(attend_kernel, out_shape=jax.ShapeDtypeStruct((DP, MSG, HD...  1.89 us

profile of v5, /device:TPU:1, one launch (start us, length us, event | category | flops | bytes accessed | tf_op | source)
XLA Modules:
  0.0 56.8 jit_solution(14854501485144070548)
XLA Ops:
  0.0 0.0 copy-start
  0.0 0.0 copy-start.5
  0.0 0.0 copy-start.3
  0.0 0.0 slice-start
  0.0 0.9 %copy-done = bf16[32,2,8,128]{3,2,1,0:T(8,128)(2,1)S(1)} copy-done((bf16[32,2,8,128]{3,2,1,0:T(8,128)(2,1)S(1)}, bf16[32,2,8,128]{3,2,1,0:T(8,128)(2,1)}, u32[]{:S(2)}) %copy-start) | copy-done | bytes 131096
  0.9 0.0 copy-done.5
  0.9 0.0 copy-done.3
  0.9 0.0 slice-start.1
  0.9 0.5 pack.1
  1.4 28.1 %all_to_all.10.in_ref = bf16[32,152,128]{2,1,0:T(8,128)(2,1)S(1)} all-to-all(bf16[32,152,128]{2,1,0:T(8,128)(2,1)S(1)} %pack.1), channel_id=1, replica_groups=mesh['dp'=32,'tensor'=8] {'dp'}, dimensions={0} | all-to-all | bytes 2490368 | tf_op jit(solution)/shard_map/all_to_all | solution.py:259
  29.4 0.0 slice-done
  29.5 0.0 slice-done.1
  29.5 1.9 %attend.1 = bf16[32,152,128]{2,1,0:T(8,128)(2,1)S(1)} custom-call(bf16[32,152,128]{2,1,0:T(8,128)(2,1)S(1)} %all_to_all.10.in_ref, bf16[40,2,256,128]{3,2,1,0:T(8,128)(2,1)S(1)} %bitcast.10), custom_call_target="tpu_custom_call" | custom-call | tf_op jit(solution)/shard_map/attend/pallas_call | solution.py:228
  31.3 0.0 copy-start.1
  31.4 0.0 copy-start.2
  31.4 0.0 copy-start.4
  31.4 23.2 %all_to_all.11.in_ref = bf16[32,152,128]{2,1,0:T(8,128)(2,1)S(1)} all-to-all(bf16[32,152,128]{2,1,0:T(8,128)(2,1)S(1)} %attend.1), channel_id=1, replica_groups=mesh['dp'=32,'tensor'=8] {'dp'}, dimensions={0} | all-to-all | bytes 2490368 | tf_op jit(solution)/shard_map/all_to_all | solution.py:259
  54.6 0.0 copy-done.1
  54.6 0.0 copy-done.2
  54.6 0.0 copy-done.4
  54.6 2.1 %combine.1 = bf16[32,16,128]{2,1,0:T(8,128)(2,1)} custom-call(s32[1,48]{1,0:T(1,128)S(1)} %bitcast.16, s32[1,32]{1,0:T(1,128)S(1)} %bitcast.17, bf16[32,152,128]{2,1,0:T(8,128)(2,1)S(1)} %all_to_all.11.in_ref, bf16[32,16,128]{2,1,0:T(8,128)(2,1)S(1)} %bitcast.12, bf16[64,128]{1,0:T(8,128)(2,1)S(1)} %bitcast.13, bf16[64,128]{1,0:T(8,128)(2,1)S(1)} %bitcast.14), custom_call_target="tpu_custom_call" | custom-call | tf_op jit(solution)/shard_map/combine/pallas_call | solution.py:247
  (2 shorter events, 0.0 us)
Async XLA Ops:
  0.0 0.9 %copy-start = (bf16[32,2,8,128]{3,2,1,0:T(8,128)(2,1)S(1)}, bf16[32,2,8,128]{3,2,1,0:T(8,128)(2,1)}, u32[]{:S(2)}) copy-start(bf16[32,2,8,128]{3,2,1,0:T(8,128)(2,1)} %param.11) | copy-start | bytes 393220
  0.0 0.9 %copy-start.5 = (s32[32]{0:T(128)S(1)}, s32[32]{0:T(128)}, u32[]{:S(2)}) copy-start(s32[32]{0:T(128)} %param.9) | copy-start | bytes 388
  0.0 0.9 %copy-start.3 = (s32[48]{0:T(128)S(1)}, s32[48]{0:T(128)}, u32[]{:S(2)}) copy-start(s32[48]{0:T(128)} %param.8) | copy-start | bytes 580
  0.0 29.4 %slice-start = ((s8[5242880]{0:T(1024)(128)(4,1)}), s8[4194304]{0:T(1024)(128)(4,1)S(1)}, s32[]{:S(2)}) async-start(s8[5242880]{0:T(1024)(128)(4,1)} %bitcast.8), calls=%async_computation.2 | async-start | bytes 8388608
  0.9 28.5 %slice-start.1 = ((s8[5242880]{0:T(1024)(128)(4,1)}), s8[1048576]{0:T(1024)(128)(4,1)S(1)}, s32[]{:S(2)}) async-start(s8[5242880]{0:T(1024)(128)(4,1)} %bitcast.8), calls=%async_computation.3 | async-start | bytes 2097152
  31.3 23.3 %copy-start.1 = (bf16[32,2,1,128]{3,1,2,0:T(2,128)(2,1)S(1)}, bf16[32,2,1,128]{3,1,2,0:T(2,128)(2,1)}, u32[]{:S(2)}) copy-start(bf16[32,2,1,128]{3,1,2,0:T(2,128)(2,1)} %param.12) | copy-start | bytes 49156
  31.4 23.3 %copy-start.2 = (bf16[32,2,1,128]{3,1,2,0:T(2,128)(2,1)S(1)}, bf16[32,2,1,128]{3,1,2,0:T(2,128)(2,1)}, u32[]{:S(2)}) copy-start(bf16[32,2,1,128]{3,1,2,0:T(2,128)(2,1)} %param.13) | copy-start | bytes 49156
  31.4 23.3 %copy-start.4 = (s32[32]{0:T(128)S(1)}, s32[32]{0:T(128)}, u32[]{:S(2)}) copy-start(s32[32]{0:T(128)} %param.10) | copy-start | bytes 388

commit v6 on v5

--- a/solution.py
+++ b/solution.py
@@ -42,21 +42,21 @@
 def pack_kernel(map_ref, len_ref, blank_ref, q_ref, out_ref, held_ref):
     row = lax.broadcasted_iota(jnp.int32, (TAIL, HD), 0)
     pages, lengths, blank = map_ref[...], len_ref[...], blank_ref[...]
+    owners = pages // POOL_ROW
+    within = pages - owners * POOL_ROW
     for s in range(DP):
         held_ref[s] = blank[0, s]
     for j in range(PROMPTS):
-        page = pages[0, j]
-        s = page // POOL_ROW
-        held_ref[s] = page - s * POOL_ROW
+        s = owners[0, j]
+        held_ref[s] = within[0, j]
         g = j // PPAGES
         for i in range(GROUP):
             out_ref[s, i * SH : (i + 1) * SH, :] = q_ref[g * GROUP + i]
     for e in range(ROWS_DEV):
-        page = pages[0, PROMPTS + e]
-        s = page // POOL_ROW
+        s = owners[0, PROMPTS + e]
         out_ref[s, BRANCH_AT:TAIL_AT, :] = q_ref[e]
         numbers = jnp.where(
-            row == 0, held_ref[s], jnp.where(row == 1, page - s * POOL_ROW, lengths[0, e])
+            row == 0, held_ref[s], jnp.where(row == 1, within[0, PROMPTS + e], lengths[0, e])
         )
         out_ref[s, TAIL_AT:MSG, :] = numbers.astype(F32).astype(BF)
 
@@ -158,8 +158,9 @@
         tail = in_ref[s, TAIL_AT:MSG, :].astype(F32)
         numbers_ref[s] = tail + pltpu.roll(tail, HD - TERM, 1) + pltpu.roll(tail, HD - 2 * TERM, 1)
 
-    pages, kept = map_ref[...], alive_ref[...]
-    holders = [pages[0, j] // POOL_ROW for j in range(PROMPTS + ROWS_DEV)]
+    pages = map_ref[...]
+    owners = pages // POOL_ROW
+    holders = [owners[0, j] for j in range(PROMPTS + ROWS_DEV)]
     blocks = []
     for k in range(PPAGES):
         block = numbers_ref[holders[k]]
@@ -181,7 +182,11 @@
     whole = wholes[0]
     for part in wholes[1:]:
         whole = whole + part
-    shares = [share / whole for share in shares]
+    kept = alive_ref[...].astype(F32)
+    unused = jnp.zeros((1, TOTAL_AT), F32)
+    kept = jnp.concatenate([kept, unused, kept, unused], axis=1)
+    kept = kept / whole
+    shares = [share * kept for share in shares]
 
     for r in range(ROWS_DEV):
         g, i = r // GROUP, r % GROUP
@@ -197,7 +202,7 @@
                 [share[:, r : r + 1], share[:, HD // 2 + r : HD // 2 + r + 1]], axis=0
             )
             result = column * part if result is None else result + column * part
-        out_ref[r] = (result * kept[0, r].astype(F32)).astype(BF)
+        out_ref[r] = result.astype(BF)
 
 
 def blank():

time: 56.9 us -> 56.5 us (level)
  no operation moved by 1% of the time
where the time goes in v6:
time: 56.5 us; the launch traced here: 56.3 us
  blocking collectives  51.3 us (91%)
  Pallas kernels  4.06 us (7%)
  local copies, waits for them, and re-layouts  0.91 us (2%)
    all_to_all x2, blocking collectives, exchange(): lax.all_to_all(message, 'dp', split_axis=0, concat_axis=0, tiled=True)  51.3 us
    pallas_call x1, Pallas kernels, attend(): pl.pallas_call(attend_kernel, out_shape=jax.ShapeDtypeStruct((DP, MSG, HD...  1.89 us
    pallas_call x1, Pallas kernels, combine(): pl.pallas_call(combine_kernel, out_shape=jax.ShapeDtypeStruct((ROWS_DEV,...  1.82 us

profile of v6, /device:TPU:1, one launch (start us, length us, event | category | flops | bytes accessed | tf_op | source)
XLA Modules:
  0.0 56.3 jit_solution(6547767801580064431)
XLA Ops:
  0.0 0.0 copy-start
  0.0 0.0 copy-start.5
  0.0 0.0 copy-start.3
  0.0 0.0 slice-start
  0.0 0.9 %copy-done = bf16[32,2,8,128]{3,2,1,0:T(8,128)(2,1)S(1)} copy-done((bf16[32,2,8,128]{3,2,1,0:T(8,128)(2,1)S(1)}, bf16[32,2,8,128]{3,2,1,0:T(8,128)(2,1)}, u32[]{:S(2)}) %copy-start) | copy-done | bytes 131096
  0.9 0.0 copy-done.5
  0.9 0.0 copy-done.3
  0.9 0.0 slice-start.1
  0.9 0.3 pack.1
  1.3 28.1 %all_to_all.10.in_ref = bf16[32,152,128]{2,1,0:T(8,128)(2,1)S(1)} all-to-all(bf16[32,152,128]{2,1,0:T(8,128)(2,1)S(1)} %pack.1), channel_id=1, replica_groups=mesh['dp'=32,'tensor'=8] {'dp'}, dimensions={0} | all-to-all | bytes 2490368 | tf_op jit(solution)/shard_map/all_to_all | solution.py:264
  29.3 0.0 slice-done
  29.3 0.0 slice-done.1
  29.3 1.9 %attend.1 = bf16[32,152,128]{2,1,0:T(8,128)(2,1)S(1)} custom-call(bf16[32,152,128]{2,1,0:T(8,128)(2,1)S(1)} %all_to_all.10.in_ref, bf16[40,2,256,128]{3,2,1,0:T(8,128)(2,1)S(1)} %bitcast.10), custom_call_target="tpu_custom_call" | custom-call | tf_op jit(solution)/shard_map/attend/pallas_call | solution.py:233
  31.2 0.0 copy-start.1
  31.2 0.0 copy-start.2
  31.3 0.0 copy-start.4
  31.3 23.2 %all_to_all.11.in_ref = bf16[32,152,128]{2,1,0:T(8,128)(2,1)S(1)} all-to-all(bf16[32,152,128]{2,1,0:T(8,128)(2,1)S(1)} %attend.1), channel_id=1, replica_groups=mesh['dp'=32,'tensor'=8] {'dp'}, dimensions={0} | all-to-all | bytes 2490368 | tf_op jit(solution)/shard_map/all_to_all | solution.py:264
  54.5 0.0 copy-done.1
  54.5 0.0 copy-done.2
  54.5 0.0 copy-done.4
  54.5 1.8 %combine.1 = bf16[32,16,128]{2,1,0:T(8,128)(2,1)} custom-call(s32[1,48]{1,0:T(1,128)S(1)} %bitcast.16, s32[1,32]{1,0:T(1,128)S(1)} %bitcast.17, bf16[32,152,128]{2,1,0:T(8,128)(2,1)S(1)} %all_to_all.11.in_ref, bf16[32,16,128]{2,1,0:T(8,128)(2,1)S(1)} %bitcast.12, bf16[64,128]{1,0:T(8,128)(2,1)S(1)} %bitcast.13, bf16[64,128]{1,0:T(8,128)(2,1)S(1)} %bitcast.14), custom_call_target="tpu_custom_call" | custom-call | tf_op jit(solution)/shard_map/combine/pallas_call | solution.py:252
  (2 shorter events, 0.0 us)
Async XLA Ops:
  0.0 0.9 %copy-start = (bf16[32,2,8,128]{3,2,1,0:T(8,128)(2,1)S(1)}, bf16[32,2,8,128]{3,2,1,0:T(8,128)(2,1)}, u32[]{:S(2)}) copy-start(bf16[32,2,8,128]{3,2,1,0:T(8,128)(2,1)} %param.11) | copy-start | bytes 393220
  0.0 0.9 %copy-start.5 = (s32[32]{0:T(128)S(1)}, s32[32]{0:T(128)}, u32[]{:S(2)}) copy-start(s32[32]{0:T(128)} %param.9) | copy-start | bytes 388
  0.0 0.9 %copy-start.3 = (s32[48]{0:T(128)S(1)}, s32[48]{0:T(128)}, u32[]{:S(2)}) copy-start(s32[48]{0:T(128)} %param.8) | copy-start | bytes 580
  0.0 29.3 %slice-start = ((s8[5242880]{0:T(1024)(128)(4,1)}), s8[4194304]{0:T(1024)(128)(4,1)S(1)}, s32[]{:S(2)}) async-start(s8[5242880]{0:T(1024)(128)(4,1)} %bitcast.8), calls=%async_computation.2 | async-start | bytes 8388608
  0.9 28.4 %slice-start.1 = ((s8[5242880]{0:T(1024)(128)(4,1)}), s8[1048576]{0:T(1024)(128)(4,1)S(1)}, s32[]{:S(2)}) async-start(s8[5242880]{0:T(1024)(128)(4,1)} %bitcast.8), calls=%async_computation.3 | async-start | bytes 2097152
  31.2 23.3 %copy-start.1 = (bf16[32,2,1,128]{3,1,2,0:T(2,128)(2,1)S(1)}, bf16[32,2,1,128]{3,1,2,0:T(2,128)(2,1)}, u32[]{:S(2)}) copy-start(bf16[32,2,1,128]{3,1,2,0:T(2,128)(2,1)} %param.12) | copy-start | bytes 49156
  31.2 23.3 %copy-start.2 = (bf16[32,2,1,128]{3,1,2,0:T(2,128)(2,1)S(1)}, bf16[32,2,1,128]{3,1,2,0:T(2,128)(2,1)}, u32[]{:S(2)}) copy-start(bf16[32,2,1,128]{3,1,2,0:T(2,128)(2,1)} %param.13) | copy-start | bytes 49156
  31.3 23.3 %copy-start.4 = (s32[32]{0:T(128)S(1)}, s32[32]{0:T(128)}, u32[]{:S(2)}) copy-start(s32[32]{0:T(128)} %param.10) | copy-start | bytes 388

commit v7 on v6

--- a/solution.py
+++ b/solution.py
@@ -61,8 +61,34 @@
         out_ref[s, TAIL_AT:MSG, :] = numbers.astype(F32).astype(BF)
 
 
+def new_tokens(q_ref, nk_ref, nv_ref, mix_ref, fresh_ref):
+    half = SH // 2
+    lane = lax.broadcasted_iota(jnp.int32, (half, HD), 1)
+    question = q_ref[...].reshape(ROWS_DEV * SH, HD)
+    scores = lax.dot_general(question, nk_ref[...], CONTRACT_LAST, preferred_element_type=F32)
+    at = lax.broadcasted_iota(jnp.int32, scores.shape, 0)
+    new = lax.broadcasted_iota(jnp.int32, scores.shape, 1)
+    usable = (at // SH == new // 2) & (new % 2 <= (at % SH) // half)
+    scores = jnp.where(usable, scores, NEG)
+    top = jnp.max(scores, axis=1, keepdims=True)
+    weights = jnp.where(usable, jnp.exp2((scores - top) * TO_LOG2), 0.0).astype(BF)
+    total = jnp.sum(weights.astype(F32), axis=1, keepdims=True)
+    mix = jnp.dot(weights, nv_ref[...], preferred_element_type=F32)
+    mix_ref[...] = mix.reshape(ROWS_DEV, SH, HD)
+    top = top * SCALE
+
+    fresh = jnp.zeros((half, HD), F32)
+    for r in range(ROWS_DEV):
+        for n, column in enumerate((top, total)):
+            for m in range(2):
+                piece = column[r * SH + m * half : r * SH + (m + 1) * half]
+                fresh = jnp.where(lane == m * HD // 2 + n * TOTAL_AT + r, piece, fresh)
+    fresh_ref[...] = fresh
+
+
 def attend_kernel(
-    in_ref, pool_ref, out_ref, numbers_s, list_s, scores_ref, weights_ref, maxima, totals
+    in_ref, pool_ref, q_ref, nk_ref, nv_ref, out_ref, mix_ref, fresh_ref,
+    numbers_s, list_s, scores_ref, weights_ref, maxima, totals
 ):
     lane = lax.broadcasted_iota(jnp.int32, (SH, HD), 1)
     token = lax.broadcasted_iota(jnp.int32, (SH, PAGE), 1)
@@ -108,6 +134,7 @@
         return carry
 
     lax.fori_loop(0, PROMPTS, prompt, 0, unroll=16)
+    new_tokens(q_ref, nk_ref, nv_ref, mix_ref, fresh_ref)
 
     highest, weights = soft(scores_ref[...])
     weights_ref[...] = weights
@@ -129,31 +156,11 @@
 
 
 def combine_kernel(
-    map_ref, alive_ref, in_ref, q_ref, nk_ref, nv_ref, out_ref, fresh_ref, numbers_ref
+    map_ref, alive_ref, in_ref, mix_ref, fresh_ref, out_ref, numbers_ref
 ):
     half = SH // 2
     lane = lax.broadcasted_iota(jnp.int32, (half, HD), 1)
     place = lane % TOTAL_AT
-    question = q_ref[...].reshape(ROWS_DEV * SH, HD)
-    scores = lax.dot_general(question, nk_ref[...], CONTRACT_LAST, preferred_element_type=F32)
-    at = lax.broadcasted_iota(jnp.int32, scores.shape, 0)
-    new = lax.broadcasted_iota(jnp.int32, scores.shape, 1)
-    usable = (at // SH == new // 2) & (new % 2 <= (at % SH) // half)
-    scores = jnp.where(usable, scores, NEG)
-    top = jnp.max(scores, axis=1, keepdims=True)
-    weights = jnp.where(usable, jnp.exp2((scores - top) * TO_LOG2), 0.0).astype(BF)
-    total = jnp.sum(weights.astype(F32), axis=1, keepdims=True)
-    mix = jnp.dot(weights, nv_ref[...], preferred_element_type=F32)
-    fresh_ref[...] = mix.reshape(ROWS_DEV, SH, HD)
-    top = top * SCALE
-
-    fresh = jnp.zeros((half, HD), F32)
-    for r in range(ROWS_DEV):
-        for n, column in enumerate((top, total)):
-            for m in range(2):
-                piece = column[r * SH + m * half : r * SH + (m + 1) * half]
-                fresh = jnp.where(lane == m * HD // 2 + n * TOTAL_AT + r, piece, fresh)
-
     for s in range(DP):
         tail = in_ref[s, TAIL_AT:MSG, :].astype(F32)
         numbers_ref[s] = tail + pltpu.roll(tail, HD - TERM, 1) + pltpu.roll(tail, HD - 2 * TERM, 1)
@@ -172,13 +179,15 @@
     for r in range(ROWS_DEV):
         own = pltpu.roll(numbers_ref[holders[PROMPTS + r]], (r - GROUP) % HD, 1)
         block = jnp.where(place == r, own, block)
-    blocks += [block, fresh]
+    blocks += [block, fresh_ref[...]]
 
     peak = blocks[0]
     for block in blocks[1:]:
         peak = jnp.maximum(peak, block)
-    shares = [jnp.exp(block - peak) for block in blocks]
-    wholes = [share * pltpu.roll(block, HD - TOTAL_AT, 1) for share, block in zip(shares, blocks)]
+    shares = [jnp.exp(block - peak).astype(BF) for block in blocks]
+    wholes = [
+        share.astype(F32) * pltpu.roll(block, HD - TOTAL_AT, 1) for share, block in zip(shares, blocks)
+    ]
     whole = wholes[0]
     for part in wholes[1:]:
         whole = whole + part
@@ -186,7 +195,11 @@
     unused = jnp.zeros((1, TOTAL_AT), F32)
     kept = jnp.concatenate([kept, unused, kept, unused], axis=1)
     kept = kept / whole
-    shares = [share * kept for share in shares]
+    kept = jnp.concatenate([kept, pltpu.roll(kept, HD // 2, 1)], axis=0)
+    shares = [
+        jnp.concatenate([share, pltpu.roll(share, HD // 2, 1)], axis=0).astype(BF)
+        for share in (share.astype(F32) for share in shares)
+    ]
 
     for r in range(ROWS_DEV):
         g, i = r // GROUP, r % GROUP
@@ -195,14 +208,12 @@
             for k in range(PPAGES)
         ]
         parts.append(in_ref[holders[PROMPTS + r], BRANCH_AT:TAIL_AT, :].astype(F32))
-        parts.append(fresh_ref[r])
+        parts.append(mix_ref[r])
         result = None
         for share, part in zip(shares, parts):
-            column = jnp.concatenate(
-                [share[:, r : r + 1], share[:, HD // 2 + r : HD // 2 + r + 1]], axis=0
-            )
+            column = jnp.broadcast_to(share[:, r : r + 1], (SH, HD)).astype(F32)
             result = column * part if result is None else result + column * part
-        out_ref[r] = result.astype(BF)
+        out_ref[r] = (result * kept[:, r : r + 1]).astype(BF)
 
 
 def blank():
@@ -229,12 +240,16 @@
     )(page_map, branch_len, blank(), question)
 
 
-def attend(asked, pages):
+def attend(asked, pages, question, new_keys, new_values):
     return pl.pallas_call(
         attend_kernel,
-        out_shape=jax.ShapeDtypeStruct((DP, MSG, HD), BF),
-        in_specs=[VMEM, VMEM],
-        out_specs=VMEM,
+        out_shape=[
+            jax.ShapeDtypeStruct((DP, MSG, HD), BF),
+            jax.ShapeDtypeStruct((ROWS_DEV, SH, HD), F32),
+            jax.ShapeDtypeStruct((SH // 2, HD), F32),
+        ],
+        in_specs=[VMEM] * 5,
+        out_specs=[VMEM] * 3,
         scratch_shapes=[
             pltpu.SMEM((3, DP), jnp.int32),
             pltpu.SMEM((DP + 8,), jnp.int32),
@@ -245,19 +260,19 @@
         ],
         compiler_params=params(20),
         name="attend",
-    )(asked, pages)
-
-
-def combine(page_map, alive, incoming, question, new_keys, new_values):
+    )(asked, pages, question, new_keys, new_values)
+
+
+def combine(page_map, alive, incoming, mix, numbers):
     return pl.pallas_call(
         combine_kernel,
         out_shape=jax.ShapeDtypeStruct((ROWS_DEV, SH, HD), BF),
-        in_specs=[VMEM, VMEM, VMEM, VMEM, VMEM, VMEM],
+        in_specs=[VMEM] * 5,
         out_specs=VMEM,
-        scratch_shapes=[pltpu.VMEM((ROWS_DEV, SH, HD), F32), pltpu.VMEM((DP, TAIL, HD), F32)],
+        scratch_shapes=[pltpu.VMEM((DP, TAIL, HD), F32)],
         compiler_params=params(20),
         name="combine",
-    )(page_map, alive, incoming, question, new_keys, new_values)
+    )(page_map, alive, incoming, mix, numbers)
 
 
 def exchange(message):
@@ -267,10 +282,12 @@
 def shards(pool, page_map, branch_len, alive, queries, new_keys, new_values):
     question = queries.reshape(ROWS_DEV, SH, HD)
     asked = exchange(pack(page_map.reshape(1, -1), branch_len.reshape(1, -1), question))
-    incoming = exchange(attend(asked, pool.reshape(POOL_ROW, 2, PAGE, HD)))
     new_keys = new_keys.reshape(ROWS_DEV * 2, HD)
     new_values = new_values.reshape(ROWS_DEV * 2, HD)
-    attended = combine(page_map.reshape(1, -1), alive.reshape(1, -1), incoming, question, new_keys, new_values)
+    pages = pool.reshape(POOL_ROW, 2, PAGE, HD)
+    answers, mix, numbers = attend(asked, pages, question, new_keys, new_values)
+    incoming = exchange(answers)
+    attended = combine(page_map.reshape(1, -1), alive.reshape(1, -1), incoming, mix, numbers)
     return attended.reshape(queries.shape)
 
 

time: 56.5 us -> 56.1 us (level)
  no operation moved by 1% of the time
where the time goes in v7:
time: 56.1 us; the launch traced here: 56 us
  blocking collectives  51.2 us (91%)
  Pallas kernels  3.84 us (7%)
  local copies, waits for them, and re-layouts  0.91 us (2%)
    all_to_all x2, blocking collectives, exchange(): lax.all_to_all(message, 'dp', split_axis=0, concat_axis=0, tiled=True)  51.2 us
    pallas_call x1, Pallas kernels, attend(): pl.pallas_call(attend_kernel, out_shape=[jax.ShapeDtypeStruct((DP, MSG, H...  2.07 us
    pallas_call x1, Pallas kernels, combine(): pl.pallas_call(combine_kernel, out_shape=jax.ShapeDtypeStruct((ROWS_DEV,...  1.41 us

profile of v7, /device:TPU:1, one launch (start us, length us, event | category | flops | bytes accessed | tf_op | source)
XLA Modules:
  0.0 56.0 jit_solution(11851404737368702186)
XLA Ops:
  0.0 0.0 copy-start
  0.0 0.0 copy-start.5
  0.0 0.0 copy-start.3
  0.0 0.0 slice-start
  0.0 0.9 %copy-done = bf16[32,2,8,128]{3,2,1,0:T(8,128)(2,1)S(1)} copy-done((bf16[32,2,8,128]{3,2,1,0:T(8,128)(2,1)S(1)}, bf16[32,2,8,128]{3,2,1,0:T(8,128)(2,1)}, u32[]{:S(2)}) %copy-start) | copy-done | bytes 131096
  0.9 0.0 copy-done.5
  0.9 0.0 copy-done.3
  0.9 0.0 slice-start.1
  0.9 0.3 pack.1
  1.3 0.0 copy-start.1
  1.3 0.0 copy-start.2
  1.3 28.1 %all_to_all.10.in_ref = bf16[32,152,128]{2,1,0:T(8,128)(2,1)S(1)} all-to-all(bf16[32,152,128]{2,1,0:T(8,128)(2,1)S(1)} %pack.1), channel_id=1, replica_groups=mesh['dp'=32,'tensor'=8] {'dp'}, dimensions={0} | all-to-all | bytes 2490368 | tf_op jit(solution)/shard_map/all_to_all | solution.py:279
  29.4 0.0 slice-done
  29.4 0.0 slice-done.1
  29.4 0.0 copy-done.1
  29.4 0.0 copy-done.2
  29.4 2.1 %attend.1 = (bf16[32,152,128]{2,1,0:T(8,128)(2,1)S(1)}, f32[32,16,128]{2,1,0:T(8,128)S(1)}, f32[8,128]{1,0:T(8,128)S(1)}) custom-call(bf16[32,152,128]{2,1,0:T(8,128)(2,1)S(1)} %all_to_all.10.in_ref, bf16[40,2,256,128]{3,2,1,0:T(8,128)(2,1)S(1)} %bitcast.10, bf16[32,16,128]{2,1,0:T(8,128)(2,1)S(1)} %bitcast.12, bf16[64,128]{1,0:T(8,128)(2,1)S(1)} %bitcast.13, ...), custom_call_target="tpu_custom_call" | custom-call | tf_op jit(solution)/shard_map/attend/pallas_call | solution.py:244
  31.5 0.0 copy-start.4
  31.5 23.1 %all_to_all.11.in_ref = bf16[32,152,128]{2,1,0:T(8,128)(2,1)S(1)} all-to-all(bf16[32,152,128]{2,1,0:T(8,128)(2,1)S(1)} %get-tuple-element.8), channel_id=1, replica_groups=mesh['dp'=32,'tensor'=8] {'dp'}, dimensions={0} | all-to-all | bytes 2490368 | tf_op jit(solution)/shard_map/all_to_all | solution.py:279
  54.6 0.0 copy-done.4
  54.6 1.4 %combine.1 = bf16[32,16,128]{2,1,0:T(8,128)(2,1)} custom-call(s32[1,48]{1,0:T(1,128)S(1)} %bitcast.16, s32[1,32]{1,0:T(1,128)S(1)} %bitcast.17, bf16[32,152,128]{2,1,0:T(8,128)(2,1)S(1)} %all_to_all.11.in_ref, f32[32,16,128]{2,1,0:T(8,128)S(1)} %get-tuple-element.9.mix_ref, f32[8,128]{1,0:T(8,128)S(1)} %get-tuple-element.10.fresh_ref), custom_call_target="tpu_custom_call" | custom-call | tf_op jit(solution)/shard_map/combine/pallas_call | solution.py:267
  (2 shorter events, 0.0 us)
Async XLA Ops:
  0.0 0.9 %copy-start = (bf16[32,2,8,128]{3,2,1,0:T(8,128)(2,1)S(1)}, bf16[32,2,8,128]{3,2,1,0:T(8,128)(2,1)}, u32[]{:S(2)}) copy-start(bf16[32,2,8,128]{3,2,1,0:T(8,128)(2,1)} %param.11) | copy-start | bytes 393220
  0.0 0.9 %copy-start.5 = (s32[32]{0:T(128)S(1)}, s32[32]{0:T(128)}, u32[]{:S(2)}) copy-start(s32[32]{0:T(128)} %param.9) | copy-start | bytes 388
  0.0 0.9 %copy-start.3 = (s32[48]{0:T(128)S(1)}, s32[48]{0:T(128)}, u32[]{:S(2)}) copy-start(s32[48]{0:T(128)} %param.8) | copy-start | bytes 580
  0.0 29.3 %slice-start = ((s8[5242880]{0:T(1024)(128)(4,1)}), s8[4194304]{0:T(1024)(128)(4,1)S(1)}, s32[]{:S(2)}) async-start(s8[5242880]{0:T(1024)(128)(4,1)} %bitcast.8), calls=%async_computation.2 | async-start | bytes 8388608
  0.9 28.4 %slice-start.1 = ((s8[5242880]{0:T(1024)(128)(4,1)}), s8[1048576]{0:T(1024)(128)(4,1)S(1)}, s32[]{:S(2)}) async-start(s8[5242880]{0:T(1024)(128)(4,1)} %bitcast.8), calls=%async_computation.3 | async-start | bytes 2097152
  1.3 28.1 %copy-start.1 = (bf16[32,2,1,128]{3,1,2,0:T(2,128)(2,1)S(1)}, bf16[32,2,1,128]{3,1,2,0:T(2,128)(2,1)}, u32[]{:S(2)}) copy-start(bf16[32,2,1,128]{3,1,2,0:T(2,128)(2,1)} %param.12) | copy-start | bytes 49156
  1.3 28.1 %copy-start.2 = (bf16[32,2,1,128]{3,1,2,0:T(2,128)(2,1)S(1)}, bf16[32,2,1,128]{3,1,2,0:T(2,128)(2,1)}, u32[]{:S(2)}) copy-start(bf16[32,2,1,128]{3,1,2,0:T(2,128)(2,1)} %param.13) | copy-start | bytes 49156
  31.5 23.1 %copy-start.4 = (s32[32]{0:T(128)S(1)}, s32[32]{0:T(128)}, u32[]{:S(2)}) copy-start(s32[32]{0:T(128)} %param.10) | copy-start | bytes 388

commit v8 on v7

--- a/solution.py
+++ b/solution.py
@@ -134,11 +134,11 @@
         return carry
 
     lax.fori_loop(0, PROMPTS, prompt, 0, unroll=16)
-    new_tokens(q_ref, nk_ref, nv_ref, mix_ref, fresh_ref)
 
     highest, weights = soft(scores_ref[...])
     weights_ref[...] = weights
     total = jnp.sum(weights.astype(F32), axis=1, keepdims=True)
+    new_tokens(q_ref, nk_ref, nv_ref, mix_ref, fresh_ref)
     for b in range(DP):
         values = pool_ref[numbers_s[1, b], 1]
         mix = jnp.dot(weights_ref[b * SH : (b + 1) * SH, :], values, preferred_element_type=F32)
@@ -209,10 +209,11 @@
         ]
         parts.append(in_ref[holders[PROMPTS + r], BRANCH_AT:TAIL_AT, :].astype(F32))
         parts.append(mix_ref[r])
-        result = None
+        terms = []
         for share, part in zip(shares, parts):
             column = jnp.broadcast_to(share[:, r : r + 1], (SH, HD)).astype(F32)
-            result = column * part if result is None else result + column * part
+            terms.append(column * part)
+        result = (terms[0] + terms[1]) + (terms[2] + terms[3]) + (terms[4] + terms[5])
         out_ref[r] = (result * kept[:, r : r + 1]).astype(BF)
 
 

time: 56.1 us -> 56.1 us (level)
  no operation moved by 1% of the time
where the time goes in v8:
time: 56.1 us; the launch traced here: 56 us
  blocking collectives  51.2 us (91%)
  Pallas kernels  3.84 us (7%)
  local copies, waits for them, and re-layouts  0.91 us (2%)
    all_to_all x2, blocking collectives, exchange(): lax.all_to_all(message, 'dp', split_axis=0, concat_axis=0, tiled=True)  51.2 us
    pallas_call x1, Pallas kernels, attend(): pl.pallas_call(attend_kernel, out_shape=[jax.ShapeDtypeStruct((DP, MSG, H...  2.07 us
    pallas_call x1, Pallas kernels, combine(): pl.pallas_call(combine_kernel, out_shape=jax.ShapeDtypeStruct((ROWS_DEV,...  1.41 us

profile of v8, /device:TPU:1, one launch (start us, length us, event | category | flops | bytes accessed | tf_op | source)
XLA Modules:
  0.0 56.0 jit_solution(4799289912108910169)
XLA Ops:
  0.0 0.0 copy-start
  0.0 0.0 copy-start.5
  0.0 0.0 copy-start.3
  0.0 0.0 slice-start
  0.0 0.9 %copy-done = bf16[32,2,8,128]{3,2,1,0:T(8,128)(2,1)S(1)} copy-done((bf16[32,2,8,128]{3,2,1,0:T(8,128)(2,1)S(1)}, bf16[32,2,8,128]{3,2,1,0:T(8,128)(2,1)}, u32[]{:S(2)}) %copy-start) | copy-done | bytes 131096
  0.9 0.0 copy-done.5
  0.9 0.0 copy-done.3
  0.9 0.0 slice-start.1
  0.9 0.3 pack.1
  1.3 0.0 copy-start.1
  1.3 0.0 copy-start.2
  1.3 28.1 %all_to_all.10.in_ref = bf16[32,152,128]{2,1,0:T(8,128)(2,1)S(1)} all-to-all(bf16[32,152,128]{2,1,0:T(8,128)(2,1)S(1)} %pack.1), channel_id=1, replica_groups=mesh['dp'=32,'tensor'=8] {'dp'}, dimensions={0} | all-to-all | bytes 2490368 | tf_op jit(solution)/shard_map/all_to_all | solution.py:280
  29.4 0.0 slice-done
  29.4 0.0 slice-done.1
  29.4 0.0 copy-done.1
  29.4 0.0 copy-done.2
  29.4 2.1 %attend.1 = (bf16[32,152,128]{2,1,0:T(8,128)(2,1)S(1)}, f32[32,16,128]{2,1,0:T(8,128)S(1)}, f32[8,128]{1,0:T(8,128)S(1)}) custom-call(bf16[32,152,128]{2,1,0:T(8,128)(2,1)S(1)} %all_to_all.10.in_ref, bf16[40,2,256,128]{3,2,1,0:T(8,128)(2,1)S(1)} %bitcast.10, bf16[32,16,128]{2,1,0:T(8,128)(2,1)S(1)} %bitcast.12, bf16[64,128]{1,0:T(8,128)(2,1)S(1)} %bitcast.13, ...), custom_call_target="tpu_custom_call" | custom-call | tf_op jit(solution)/shard_map/attend/pallas_call | solution.py:245
  31.5 0.0 copy-start.4
  31.5 23.1 %all_to_all.11.in_ref = bf16[32,152,128]{2,1,0:T(8,128)(2,1)S(1)} all-to-all(bf16[32,152,128]{2,1,0:T(8,128)(2,1)S(1)} %get-tuple-element.8), channel_id=1, replica_groups=mesh['dp'=32,'tensor'=8] {'dp'}, dimensions={0} | all-to-all | bytes 2490368 | tf_op jit(solution)/shard_map/all_to_all | solution.py:280
  54.6 0.0 copy-done.4
  54.6 1.4 %combine.1 = bf16[32,16,128]{2,1,0:T(8,128)(2,1)} custom-call(s32[1,48]{1,0:T(1,128)S(1)} %bitcast.16, s32[1,32]{1,0:T(1,128)S(1)} %bitcast.17, bf16[32,152,128]{2,1,0:T(8,128)(2,1)S(1)} %all_to_all.11.in_ref, f32[32,16,128]{2,1,0:T(8,128)S(1)} %get-tuple-element.9.mix_ref, f32[8,128]{1,0:T(8,128)S(1)} %get-tuple-element.10.fresh_ref), custom_call_target="tpu_custom_call" | custom-call | tf_op jit(solution)/shard_map/combine/pallas_call | solution.py:268
  (2 shorter events, 0.0 us)
Async XLA Ops:
  0.0 0.9 %copy-start = (bf16[32,2,8,128]{3,2,1,0:T(8,128)(2,1)S(1)}, bf16[32,2,8,128]{3,2,1,0:T(8,128)(2,1)}, u32[]{:S(2)}) copy-start(bf16[32,2,8,128]{3,2,1,0:T(8,128)(2,1)} %param.11) | copy-start | bytes 393220
  0.0 0.9 %copy-start.5 = (s32[32]{0:T(128)S(1)}, s32[32]{0:T(128)}, u32[]{:S(2)}) copy-start(s32[32]{0:T(128)} %param.9) | copy-start | bytes 388
  0.0 0.9 %copy-start.3 = (s32[48]{0:T(128)S(1)}, s32[48]{0:T(128)}, u32[]{:S(2)}) copy-start(s32[48]{0:T(128)} %param.8) | copy-start | bytes 580
  0.0 29.3 %slice-start = ((s8[5242880]{0:T(1024)(128)(4,1)}), s8[4194304]{0:T(1024)(128)(4,1)S(1)}, s32[]{:S(2)}) async-start(s8[5242880]{0:T(1024)(128)(4,1)} %bitcast.8), calls=%async_computation.2 | async-start | bytes 8388608
  0.9 28.4 %slice-start.1 = ((s8[5242880]{0:T(1024)(128)(4,1)}), s8[1048576]{0:T(1024)(128)(4,1)S(1)}, s32[]{:S(2)}) async-start(s8[5242880]{0:T(1024)(128)(4,1)} %bitcast.8), calls=%async_computation.3 | async-start | bytes 2097152
  1.3 28.1 %copy-start.1 = (bf16[32,2,1,128]{3,1,2,0:T(2,128)(2,1)S(1)}, bf16[32,2,1,128]{3,1,2,0:T(2,128)(2,1)}, u32[]{:S(2)}) copy-start(bf16[32,2,1,128]{3,1,2,0:T(2,128)(2,1)} %param.12) | copy-start | bytes 49156
  1.3 28.1 %copy-start.2 = (bf16[32,2,1,128]{3,1,2,0:T(2,128)(2,1)S(1)}, bf16[32,2,1,128]{3,1,2,0:T(2,128)(2,1)}, u32[]{:S(2)}) copy-start(bf16[32,2,1,128]{3,1,2,0:T(2,128)(2,1)} %param.13) | copy-start | bytes 49156
  31.5 23.1 %copy-start.4 = (s32[32]{0:T(128)S(1)}, s32[32]{0:T(128)}, u32[]{:S(2)}) copy-start(s32[32]{0:T(128)} %param.10) | copy-start | bytes 388
